TPU v7x, 32 devices: a whole 2x2x4 slice. The times are simulated.
32 devices in a mesh: seq: 16 (over z, y, x), tp: 2 (over core).
Axes of the slice: x: 2, y: 2, z: 4, core: 2. Of those that a mesh axis runs over, the one named last changes fastest.
Arguments:
- tokens: bfloat16 [16384, 1024], P(('seq', 'tp')), may hold values from -6 to 6
- norm_gain: float32 [1024], replicated, may hold values from 0.5 to 1.5
- query_weight: bfloat16 [1024, 1024], P(None, 'tp'), may hold values from -0.1875 to 0.1875
- key_weight: bfloat16 [1024, 1024], P(None, 'tp'), may hold values from -0.1875 to 0.1875
- value_weight: bfloat16 [1024, 1024], P(None, 'tp'), may hold values from -0.1875 to 0.1875
- forget_weight: bfloat16 [1024, 256], P(None, 'tp'), may hold values from -0.09375 to 0.09375
- forget_bias: float32 [256], P('tp'), may hold values from 1 to 10
- head_gain: float32 [1024], P('tp'), may hold values from 0.5 to 1.5
- out_weight: bfloat16 [1024, 1024], P('tp'), may hold values from -0.1875 to 0.1875
- feed_gain: float32 [1024], replicated, may hold values from 0.5 to 1.5
- gate_weight: bfloat16 [1024, 2816], P(None, 'tp'), may hold values from -0.1875 to 0.1875
- up_weight: bfloat16 [1024, 2816], P(None, 'tp'), may hold values from -0.1875 to 0.1875
- down_weight: bfloat16 [2816, 1024], P('tp'), may hold values from -0.109375 to 0.109375
- lengths: int32 [4], replicated, may hold values from 1 to 15424, as said below
- cotangent: bfloat16 [16384, 1024], P(('seq', 'tp')), may hold values from -6 to 6
Outputs:
- block_out: bfloat16 [16384, 1024], P(('seq', 'tp'))
- tokens_grad: bfloat16 [16384, 1024], P(('seq', 'tp'))
- norm_gain_grad: float32 [1024], replicated
- query_weight_grad: float32 [1024, 1024], P(None, 'tp')
- key_weight_grad: float32 [1024, 1024], P(None, 'tp')
- value_weight_grad: float32 [1024, 1024], P(None, 'tp')
- forget_weight_grad: float32 [1024, 256], P(None, 'tp')
- forget_bias_grad: float32 [256], P('tp')
- head_gain_grad: float32 [1024], P('tp')
- out_weight_grad: float32 [1024, 1024], P('tp')
- feed_gain_grad: float32 [1024], replicated
- gate_weight_grad: float32 [1024, 2816], P(None, 'tp')
- up_weight_grad: float32 [1024, 2816], P(None, 'tp')
- down_weight_grad: float32 [2816, 1024], P('tp')
Inputs may be any that keep to these rules, and one draw needn't show every extreme that they name: `lengths`: every length lies between 64 * (k - 1) + 1 and 64 * k for its bucket count k; the buckets of all 4 sequences fill all 16384 positions exactly; exactly one length is 15424, the others take 1024 - 64 positions of buckets together.
All inputs are finite; a program needn't handle non-finite values.
Results may differ from a plain program's by a relative error of at most 0.023.
Values may be sent and summed in bfloat16 or wider, within the bound.
A program may use at most 192 MiB of HBM per device.

v0:
```python
import functools

import jax
import jax.numpy as jnp
import numpy as np
from jax import lax
from jax.experimental import pallas as pl
from jax.experimental.pallas import tpu as pltpu
from jax.sharding import PartitionSpec as P

DH = 256
SLOTS = 64
BUCKET = 64
CH = 128
BASE = 8
HALVES = (64, 32, 16, 8)
RESET_LOG = -16384.0
LIFT = 2.0**20
SCALE = DH**-0.5

EPS = 1e-06
NORMALIZER = 8.0

BF = jnp.bfloat16
F32 = jnp.float32
VMEM_LIMIT = 56 * 1024 * 1024
UNIT = 1024
MESH = pl.DeviceIdType.MESH


def dot(a, b):
    return lax.dot_general(a, b, (((1,), (0,)), ((), ())), preferred_element_type=F32)


def nt(a, b):
    return lax.dot_general(a, b, (((1,), (1,)), ((), ())), preferred_element_type=F32)


def tn(a, b):
    return lax.dot_general(a, b, (((0,), (0,)), ((), ())), preferred_element_type=F32)


def tables():
    t, u = np.arange(CH)[:, None], np.arange(CH)[None, :]
    sums, pairs = [u <= t, u > t], []
    for half in HALVES:
        mid = t // (2 * half) * (2 * half) + half
        sums.append(np.where(t >= mid, (u >= mid) & (u <= t), (u > t) & (u < mid)))
        pairs.append(
            (t // (2 * half) == u // (2 * half)) & (t % (2 * half) >= half) & (u % (2 * half) < half)
        )
    ref = t // BASE * BASE + BASE // 2 - 1
    sums.append(((u > ref) & (u <= t)).astype(int) - ((u > t) & (u <= ref)).astype(int))
    pairs.append((t // BASE == u // BASE) & (u <= t))
    stacked = np.concatenate([s.astype(np.float32) for s in sums], 0)
    return (
        np.concatenate([stacked] * 3, 1),
        np.stack(pairs).astype(np.float32),
        np.stack([p.T for p in pairs]).astype(np.float32),
        np.concatenate([stacked.T] * 2, 1),
    )


def split3(x):
    high = x.astype(BF)
    rest = x - high.astype(F32)
    middle = rest.astype(BF)
    low = (rest - middle.astype(F32)).astype(BF)
    return jnp.concatenate([high, middle, low], 0)


def split2(x):
    high = x.astype(BF)
    return jnp.concatenate([high, (x - high.astype(F32)).astype(BF)], 0)


def decays(gate, weight, sums_ref):
    sums = dot(sums_ref[...], split3(gate))
    part = [sums[i * CH : (i + 1) * CH] for i in range(3 + len(HALVES))]
    first, last = jnp.exp(part[0]), jnp.exp(part[1])
    rows = [jnp.exp(p) for p in part[2:-1]]
    cols = [r * weight for r in rows]
    slopes = list(rows)
    rows.append(jnp.exp(part[-1]) * LIFT)
    slopes.append(jnp.exp(-part[-1]) * (1 / LIFT))
    cols.append(slopes[-1] * weight)
    return first, last, rows, cols, slopes


def halves(x):
    left = lax.broadcasted_iota(jnp.int32, x.shape, 1) < SLOTS
    zero = jnp.zeros_like(x)
    return jnp.where(left, x, zero), jnp.where(left, zero, x)


def head(x, h):
    return x[:, h * DH : (h + 1) * DH]


def slots(x, h):
    return x[:, h * SLOTS : (h + 1) * SLOTS]


def state(x, h):
    return x[h * SLOTS : (h + 1) * SLOTS]


def through(pairwise, rows, cols, pairs_ref):
    total = None
    for i in range(len(rows)):
        keep = pairs_ref[i].astype(F32) != 0
        left = jnp.concatenate([jnp.where(keep, p, 0.0).astype(BF) for p in pairwise], 1)
        right = jnp.concatenate(halves(cols[i].astype(BF)), 0)
        term = rows[i] * dot(left, right)
        total = term if total is None else total + term
    return total


def back_through(values, rows, cols, pairs_ref):
    totals = None
    for i in range(len(rows)):
        keep = pairs_ref[i].astype(F32) != 0
        stack = [part for v in values for part in halves((v * rows[i]).astype(BF))]
        out = nt(jnp.concatenate(stack, 0), cols[i].astype(BF))
        terms = [jnp.where(keep, out[n * CH : (n + 1) * CH], 0.0) for n in range(len(stack))]
        totals = terms if totals is None else [a + b for a, b in zip(totals, terms)]
    return totals


def softmax2(logits):
    out = []
    for h in range(2):
        x = slots(logits, h) * SCALE
        e = jnp.exp(x - jnp.max(x, axis=-1, keepdims=True))
        out.append(e / jnp.sum(e, axis=-1, keepdims=True))
    return jnp.concatenate(out, 1)


def fade_of(gate):
    return jnp.exp(jnp.sum(gate.T, axis=1, keepdims=True))


def run_part(trail, keys, values):
    return jnp.concatenate(
        [
            jnp.concatenate([tn(slots(trail, h), head(keys, h)), tn(slots(trail, h), head(values, h))], 1)
            for h in range(2)
        ],
        0,
    )


def state_grads(dl, probs, first, q, dmix):
    a, b = (dl * first).astype(BF), (probs * first).astype(BF)
    return jnp.concatenate(
        [jnp.concatenate([tn(slots(a, h), head(q, h)), tn(slots(b, h), head(dmix, h))], 1) for h in range(2)], 0
    )


def line_sizes(count):
    return {16: (2, 2, 4), 64: (4, 4, 4)}.get(count, (count, 1, 1))


class Lines:
    def __init__(self, sizes):
        self.sizes = sizes
        self.index = lax.axis_index("seq")
        self.half = lax.axis_index("tp")
        self.strides = (1, sizes[0], sizes[0] * sizes[1])
        self.place = [lax.rem(self.index // s, m) for s, m in zip(self.strides, sizes)]

    def peer(self, axis, d):
        m = self.sizes[axis]
        return self.index + (lax.rem(self.place[axis] + d, m) - self.place[axis]) * self.strides[axis]

    def greet(self):
        barrier = pltpu.get_barrier_semaphore()
        count = 1
        pl.semaphore_signal(barrier, inc=1, device_id={"tp": 1 - self.half}, device_id_type=MESH)
        for axis in range(3):
            for d in range(1, self.sizes[axis]):
                pl.semaphore_signal(barrier, inc=1, device_id={"seq": self.peer(axis, d)}, device_id_type=MESH)
                count += 1
        pl.semaphore_wait(barrier, count)


def remote(src, dst, sems, at, device):
    return pltpu.make_async_remote_copy(
        src_ref=src, dst_ref=dst, send_sem=sems[0].at[at], recv_sem=sems[1].at[at], device_id=device, device_id_type=MESH
    )


def job_scratch(sizes, jobs, inside):
    scratch = []
    for a, _, units, order in jobs:
        rows = UNIT
        if not inside[a]:
            scratch.append(pltpu.VMEM((units, UNIT // sizes[order[0]], 128), BF))
        for axis in order:
            rows = rows // sizes[axis]
            scratch.append(pltpu.VMEM((max(sizes[axis] - 1, 1), units, rows, 128), BF))
    most = max(max(sizes) - 1, 1)
    return scratch + [pltpu.SemaphoreType.DMA((len(jobs), 6, most))] * 2 + [pltpu.SemaphoreType.DMA((len(jobs), 2))]


class Jobs:
    def __init__(self, lines, jobs, ins, outs, inside, scratch):
        self.lines, self.jobs, self.ins, self.outs, self.inside = lines, jobs, ins, outs, inside
        self.sems, self.local = scratch[-3:-1], scratch[-1]
        self.mine, self.held, self.got, self.shape = [], [], [], []
        scratch = list(scratch)
        for j, (a, _, _, order) in enumerate(jobs):
            rows, offset, shape = UNIT, 0, []
            for axis in order:
                rows = rows // lines.sizes[axis]
                mine = lines.place[axis] * rows
                offset = offset + mine
                shape.append((axis, rows, pl.multiple_of(mine, 16), pl.multiple_of(offset, 16)))
            self.shape.append(shape)
            self.mine.append(None if inside[a] else scratch.pop(0))
            self.got.append([scratch.pop(0) for _ in range(3)])
            self.held.append([got.at[0] for got in self.got[j]])

    def copies(self, j, s):
        lines, (a, first, units, _) = self.lines, self.jobs[j]
        stage = s if s < 3 else 5 - s
        axis, rows, _, offset = self.shape[j][stage]
        out = []
        for d in range(1, lines.sizes[axis]):
            if s < 3:
                target = pl.multiple_of(lax.rem(lines.place[axis] + d, lines.sizes[axis]) * rows, 16)
                if s == 0:
                    src = self.ins[a].at[pl.ds(first, units), pl.ds(target, rows), :]
                else:
                    src = self.held[j][s - 1].at[:, pl.ds(target, rows), :]
                dst = self.got[j][s].at[d - 1]
            else:
                dst = self.outs[a].at[pl.ds(first, units), pl.ds(offset, rows), :]
                src = self.held[j][2] if s == 3 else dst
            out.append(remote(src, dst, self.sems, (j, s, d - 1), {"seq": lines.peer(axis, d)}))
        return out

    def own(self, j):
        a, first, units, _ = self.jobs[j]
        _, rows, mine, _ = self.shape[j][0]
        src = self.ins[a].at[pl.ds(first, units), pl.ds(mine, rows), :]
        return pltpu.make_async_copy(src, self.mine[j], self.local.at[j, 0])

    def home(self, j):
        a, first, units, _ = self.jobs[j]
        _, rows, _, offset = self.shape[j][2]
        dst = self.outs[a].at[pl.ds(first, units), pl.ds(offset, rows), :]
        return pltpu.make_async_copy(self.held[j][2], dst, self.local.at[j, 1])

    def add(self, j, stage):
        a, first, units, _ = self.jobs[j]
        axis, rows, mine, _ = self.shape[j][stage]
        held, got = self.held[j], self.got[j]

        def one(u, carry):
            if stage > 0:
                total = held[stage - 1][u, pl.ds(mine, rows), :].astype(F32)
            elif self.inside[a]:
                total = self.ins[a][first + u, pl.ds(mine, rows), :].astype(F32)
            else:
                total = self.mine[j][u].astype(F32)
            for d in range(self.lines.sizes[axis] - 1):
                total = total + got[stage][d, u].astype(F32)
            held[stage][u] = total.astype(BF)
            return carry

        lax.fori_loop(0, units, one, 0)

    def step(self, j, s):
        if s == 0 and not self.inside[self.jobs[j][0]]:
            self.own(j).start()
        if s == 1 and not self.inside[self.jobs[j][0]]:
            self.own(j).wait()
        if s == 4:
            self.home(j).wait()
        if s > 0:
            for copy in self.copies(j, s - 1):
                copy.wait_recv()
        if 1 <= s <= 3:
            self.add(j, s - 1)
        if s == 3:
            self.home(j).start()
        if s < 6:
            for copy in self.copies(j, s):
                copy.start()

    def finish(self):
        for j in range(len(self.jobs)):
            for s in range(6):
                for copy in self.copies(j, s):
                    copy.wait_send()


def scan_lines(lines, total_ref, fade_ref, enter_ref, reach_ref, sent_ref, got_ref, sems, earlier, between):
    width = total_ref.shape[1]
    enter_ref[...] = jnp.zeros_like(enter_ref)
    reach_ref[...] = jnp.ones_like(reach_ref)
    count = lines.sizes[0] * lines.sizes[1] * lines.sizes[2]
    rounds = count.bit_length() - 1
    side = [lax.rem(lines.index // (1 << bit), 2) for bit in range(rounds)]

    def copy(bit):
        partner = lines.index + (1 - 2 * side[bit]) * (1 << bit)
        return remote(sent_ref.at[bit], got_ref.at[bit], sems, bit, {"seq": partner})

    for bit in range(rounds):
        fade = fade_ref[...]
        high = fade.astype(BF)
        sent_ref[bit, :, :width] = total_ref[...].astype(BF)
        sent_ref[bit, :, width : width + CH] = high
        sent_ref[bit, :, width + CH :] = (fade - high.astype(F32)).astype(BF)
        copy(bit).start()
        between(bit)
        copy(bit).wait_recv()
        part = got_ref[bit, :, :width].astype(F32)
        part_fade = got_ref[bit, :, width : width + CH].astype(F32) + got_ref[bit, :, width + CH :].astype(F32)
        behind = side[bit] == (1 if earlier else 0)
        enter, reach, total = enter_ref[...], reach_ref[...], total_ref[...]
        enter_ref[...] = jnp.where(behind, reach[:, :1] * part + enter, enter)
        reach_ref[...] = jnp.where(behind, reach * part_fade, reach)
        total_ref[...] = jnp.where(behind, fade[:, :1] * part + total, part_fade[:, :1] * total + part)
        fade_ref[...] = fade * part_fade
    return [copy(bit) for bit in range(rounds)]


def chunk_rows(c):
    return pl.ds(pl.multiple_of(c * CH, CH), CH)


def score_chunk(c, s):
    at = chunk_rows(c)
    dnormed = nt(s.da[at], s.wo[...])
    dnormed = jnp.where(s.code[at, :1] > 0.5, dnormed, 0.0)
    dmix = []
    for h in range(2):
        mixed = s.mixed[at, h * DH : (h + 1) * DH]
        r = lax.rsqrt(jnp.mean(mixed * mixed, axis=-1, keepdims=True) + EPS)
        n = mixed * r
        d = head(dnormed, h)
        u = d * s.gain[:, h * DH : (h + 1) * DH]
        s.gain_grad[:, h * DH : (h + 1) * DH] += jnp.sum(d * n, axis=0, keepdims=True)
        dmix.append(r * (u - n * jnp.mean(u * n, axis=-1, keepdims=True)))
    wide = jnp.concatenate(dmix, 1)
    dmix = wide.astype(BF)
    s.dmix[at] = dmix
    rest = (wide - dmix.astype(F32)).astype(BF)
    exact = [jnp.concatenate([head(dmix, h), head(rest, h)], 0) for h in range(2)]
    q, v = s.q[at], s.v[at]
    gate, weight = s.gate[at], s.weight[at]
    first, _, rows, cols, _ = decays(gate, weight, s.sums)
    logits = s.logits[at]
    probs = softmax2(logits)
    low = s.kvs[c]
    fold = lambda x: x[:CH] + x[CH:]
    reads = [fold(nt(exact[h], head(v, h))) for h in range(2)]
    outer = jnp.concatenate([fold(nt(exact[h], state(low, h)[:, DH:])) for h in range(2)], 1)
    dprobs = first * outer + through(reads, rows, cols, s.pairs)
    weighted = probs * dprobs
    sums = [
        jnp.broadcast_to(jnp.sum(slots(weighted, h), axis=-1, keepdims=True), (CH, SLOTS)) for h in range(2)
    ]
    dl = (weighted - probs * jnp.concatenate(sums, 1)) * SCALE
    s.dl[at] = dl
    part = state_grads(dl, probs, first, q, dmix)
    reach = s.fade[...]
    s.dkv[...] += jnp.concatenate([reach] * (s.dkv.shape[1] // reach.shape[1]), 1) * part
    s.fade[...] = reach * fade_of(gate)


def grad_chunk(c, s):
    at = chunk_rows(c)
    q, k, v, dmix = s.q[at], s.k[at], s.v[at], s.dmix[at]
    gate, weight = s.gate[at], s.weight[at]
    dl = s.dl[at]
    first, last, rows, cols, slopes = decays(gate, weight, s.sums)
    probs = softmax2(s.logits[at])
    low, dkv = s.kvs[c], s.enter[...]
    dlow = dkv.astype(BF)
    r0, r1, s0, s1 = back_through([probs, dl], rows, cols, s.pairs)
    turned = [nt(head(a, h), head(b, h)) for h in range(2) for a, b in ((k, q), (v, dmix))]
    dw = last * jnp.concatenate(
        [nt(jnp.concatenate([head(k, h), head(v, h)], 1), state(dlow, h)) for h in range(2)], 1
    )
    parts = [None, weight * dw]
    scores = [nt(head(q, h), head(k, h)) for h in range(2)]
    reads = [nt(head(dmix, h), head(v, h)) for h in range(2)]
    outer = [
        jnp.concatenate([nt(head(x, h), state(low, h)[:, at_state]) for h in range(2)], 1)
        for x, at_state in ((q, slice(0, DH)), (dmix, slice(DH, 2 * DH)))
    ]
    parts[0] = first * (dl * outer[0] + probs * outer[1])
    for i in range(len(rows)):
        keep = s.flipped[i].astype(F32) != 0
        left = jnp.concatenate([jnp.where(keep, x, 0.0).astype(BF) for x in turned], 1)
        a, b = halves((dl * rows[i]).astype(BF)), halves((probs * rows[i]).astype(BF))
        late = slopes[i] * dot(left, jnp.concatenate([a[0], b[0], a[1], b[1]], 0))
        dw = dw + late
        keep = s.pairs[i].astype(F32) != 0
        left = [jnp.concatenate([jnp.where(keep, x, 0.0).astype(BF) for x in both], 1) for both in (scores, reads)]
        early = dot(jnp.concatenate(left, 0), jnp.concatenate(halves(cols[i].astype(BF)), 0))
        early = rows[i] * (dl * early[:CH] + probs * early[CH:])
        parts.append(early + weight * late if i < len(HALVES) else early - weight * late)
    trail = (last * weight).astype(BF)
    spread = (dl * first).astype(BF)
    reading, dscore = [r0.astype(BF), r1.astype(BF)], [s0.astype(BF), s1.astype(BF)]
    dq, dk, dv = [], [], []
    for h in range(2):
        dq.append(dot(dscore[h], head(k, h)) + dot(slots(spread, h), state(low, h)[:, :DH]))
        dk.append(tn(dscore[h], head(q, h)) + dot(slots(trail, h), state(dlow, h)[:, :DH]))
        dv.append(tn(reading[h], head(dmix, h)) + dot(slots(trail, h), state(dlow, h)[:, DH:]))
    dq = (jnp.concatenate(dq, 1) * s.dsq[at].astype(F32)).astype(BF)
    dk = (jnp.concatenate(dk, 1) * s.dsk[at].astype(F32)).astype(BF)
    dv = jnp.concatenate(dv, 1).astype(BF)
    fade = fade_of(gate)
    across = jnp.sum(fade * low.astype(F32) * dkv, axis=1, keepdims=True)
    across = jnp.broadcast_to(across, (across.shape[0], CH)).T[:1]
    flow = dot(s.back[...], split2(jnp.concatenate(parts, 0))) + across
    df = ((flow - jnp.exp(gate) * dw) * s.dzf[at]).astype(BF)
    s.d_all[at] = jnp.concatenate([dq, dk, dv, df], 1)
    s.bias_grad[...] += jnp.sum(df.astype(F32), axis=0, keepdims=True)
    s.enter[...] = fade * dkv + state_grads(dl, probs, first, q, dmix)
    dx = nt(dq, s.wq[...]) + nt(dk, s.wk[...]) + nt(dv, s.wv[...]) + nt(df, s.wf[...])
    s.norm_grad[...] += jnp.sum(dx * s.xn[at].astype(F32), axis=0, keepdims=True)
    s.dx[at] = dx.astype(BF)


class Bag:
    pass


LOADED = (
    "wo", "mixed", "code", "gain", "q", "k", "v", "gate", "weight", "logits", "kvs", "sums", "pairs", "flipped", "back",
    "dsq", "dsk", "dzf", "wq", "wk", "wv", "wf", "normed", "norm_gain", "feed_gain",
)


FF_STEPS = ((0, 1), (2, 3), (4,), (5,))
INSIDE = (True, True, True, True)
ROWS = 128


def back_kernel(sizes, jobs, ticks, pieces, *refs):
    refs = list(refs)
    take = lambda n: [refs.pop(0) for _ in range(n)]
    dh_own, dh_got, act, cot, hn, dgate, dup, down_weight, resid, tokens, xn = take(11)
    sources = take(len(LOADED))
    gains_out, bias_out, head_out, block_out, tokens_out, feed_got, dx_got, dresid, *outs = take(12)
    s = Bag()
    for name in LOADED:
        setattr(s, name, refs.pop(0))
    for name in ("hn", "da", "dmix", "dl", "wide_grads", "gain_grad", "bias_grad", "norm_grad", "dkv", "fade", "enter",
                 "reach", "ff_units", "down_units", "mixer_units", "out_units", "feed_part", "sent", "got", "small_held", "small_got",
                 "wide", "narrow", "result"):
        setattr(s, name, refs.pop(0))
    s.dx = s.da
    hidden = dgate.shape[1]
    s.dgate, s.dup = s.wide_grads.at[:, :hidden], s.wide_grads.at[:, hidden:]
    s.d_all = s.wide_grads.at[:, : 3 * s.wq.shape[1] + s.wf.shape[1]]
    load_sem, row_sem, piece_sem, feed_sem = take(4)
    scan_sems, small_sems, swap_sems = take(2), take(2), take(2)
    lines = Lines(sizes)
    half, width = dh_own.shape
    count = 2 * half // CH
    tp_peer = {"tp": 1 - lines.half}

    other_rows = pl.ds(pl.multiple_of((1 - lines.half) * half, half), half)
    early = [
        pltpu.make_async_copy(act, s.wide_grads.at[:, :hidden], row_sem.at[0]),
        pltpu.make_async_copy(cot, s.wide_grads.at[:, hidden : hidden + width], row_sem.at[1]),
    ]
    loads = [pltpu.make_async_copy(x, getattr(s, n), load_sem.at[i]) for i, (n, x) in enumerate(zip(LOADED, sources))]
    late = [
        pltpu.make_async_copy(hn, s.hn, row_sem.at[2]),
        pltpu.make_async_copy(dgate, s.dgate, row_sem.at[3]),
        pltpu.make_async_copy(dup, s.dup, row_sem.at[4]),
    ]
    for copy in early + loads + late[:1]:
        copy.start()
    for ref in (s.gain_grad, s.bias_grad, s.norm_grad, s.feed_part, s.dkv):
        ref[...] = jnp.zeros_like(ref)
    s.fade[...] = jnp.ones_like(s.fade)
    lines.greet()
    dx_swap = remote(s.dx.at[other_rows], dx_got, swap_sems, 0, tp_peer)
    work = Jobs(
        lines, jobs, [s.ff_units, s.down_units, s.mixer_units, s.out_units], outs, INSIDE, refs
    )
    pending = [list(t) for t in ticks]

    def tick():
        for j, step in pending.pop(0):
            work.step(j, step)

    def loop(body):
        todo = [pending.pop(0) for _ in range(count)]

        def one(i, carry):
            body(i)
            for k, steps in enumerate(todo):
                if steps:

                    @pl.when(i == k)
                    def _():
                        for j, step in steps:
                            work.step(j, step)

            return carry

        lax.fori_loop(0, count, one, 0)

    for copy in early:
        copy.wait()

    def down_part(n):
        part = tn(s.wide_grads[:, :hidden], s.wide_grads[:, hidden + n * 256 : hidden + (n + 1) * 256]).astype(BF)
        for c in range(2):
            row, done = (2 * n + c) * hidden, 0
            while done < hidden:
                some = min(hidden - done, UNIT - (row + done) % UNIT)
                at = (row + done) % UNIT
                s.down_units[(row + done) // UNIT, at : at + some] = part[done : done + some, c * 128 : (c + 1) * 128]
                done += some

    def row_loads(n):
        at, slot = pl.ds(n * ROWS, ROWS), n % 2
        return [
            pltpu.make_async_copy(src.at[at], dst, piece_sem.at[n, 8 + i])
            for i, (src, dst) in enumerate(
                ((resid, s.wide.at[slot]), (dh_own, s.narrow.at[slot]), (dh_got, s.narrow.at[2 + slot]))
            )
        ]

    def mine(n):
        return pl.ds(pl.multiple_of(lines.half * half + n * ROWS, ROWS), ROWS)

    def dresid_save(n):
        return pltpu.make_async_copy(s.wide.at[n % 2], dresid.at[pl.ds(n * ROWS, ROWS)], piece_sem.at[n, 11])

    def row_grads(n):
        slot = n % 2
        for copy in row_loads(n):
            copy.wait()
        x = s.wide[slot]
        r = lax.rsqrt(jnp.mean(x * x, axis=-1, keepdims=True) + EPS)
        norm = x * r
        dh = s.narrow[slot].astype(F32) + s.narrow[2 + slot].astype(F32)
        s.feed_part[...] += jnp.sum(dh * norm, axis=0, keepdims=True)
        u = dh * s.feed_gain[...]
        full = s.wide_grads[n * ROWS : (n + 1) * ROWS, hidden : hidden + width].astype(F32)
        full = full + r * (u - norm * jnp.mean(u * norm, axis=-1, keepdims=True))
        s.wide[slot] = full
        s.da[mine(n)] = full.astype(BF)
        dresid_save(n).start()

    steps = half // ROWS
    da_swaps = [remote(s.da.at[mine(n)], s.da.at[mine(n)], swap_sems, 1 + n, tp_peer) for n in range(steps)]
    for n in range(2):
        for copy in row_loads(n):
            copy.start()
    for copy in loads:
        copy.wait()
    for n in range(steps):
        row_grads(n)
        da_swaps[n].start()
        down_part(n)
        dresid_save(n).wait()
        if n + 2 < steps:
            for copy in row_loads(n + 2):
                copy.start()
        tick()
    for copy in late[1:]:
        copy.start()
    for copy in da_swaps:
        copy.wait_recv()
    loop(lambda i: score_chunk(i, s))
    for copy in da_swaps:
        copy.wait_send()
    for copy in late:
        copy.wait()

    def out_part(n):
        wide = width // 4
        part = tn(s.normed[...], s.da[:, n * wide : (n + 1) * wide]).astype(BF)
        tall = part.shape[0]
        for c in range(wide // 128):
            row = (n * (wide // 128) + c) * tall
            s.out_units[row // UNIT, row % UNIT : row % UNIT + tall] = part[:, c * 128 : (c + 1) * 128]

    def ff_part(n):
        at = slice(n * 256, min((n + 1) * 256, s.dgate.shape[1]))
        part = tn(s.hn[...], jnp.concatenate([s.dgate[:, at], s.dup[:, at]], 1)).astype(BF)
        for c in range(part.shape[1] // 128):
            s.ff_units[4 * n + c] = part[:, c * 128 : (c + 1) * 128]

    def between(n):
        if n < 4:
            out_part(n)
            for m in FF_STEPS[n]:
                ff_part(m)
            if n == 3:
                xn_load.start()
            tick()

    xn_load = pltpu.make_async_copy(xn, s.hn, row_sem.at[5])

    scans = scan_lines(lines, s.dkv, s.fade, s.enter, s.reach, s.sent, s.got, scan_sems, False, between)
    xn_load.wait()
    s.xn = s.hn
    loop(lambda i: grad_chunk(count - 1 - i, s))
    dx_swap.start()

    lanes = s.bias_grad.shape[1]
    vectors = [s.norm_grad[...] / s.norm_gain[...], s.feed_part[...], s.bias_grad[...], s.gain_grad[...]]
    row = 0
    for v in vectors:
        for c in range(v.shape[1] // lanes):
            s.small_held[0, row : row + 1] = v[:, c * lanes : (c + 1) * lanes]
            row += 1
    s.small_held[0, row:] = jnp.zeros_like(s.small_held[0, row:])

    def small_copies(n):
        if n == 3:
            return [remote(s.small_held.at[3], s.small_got.at[3, 0], small_sems, (3, 0), tp_peer)]
        return [
            remote(s.small_held.at[n], s.small_got.at[n, d - 1], small_sems, (n, d - 1), {"seq": lines.peer(n, d)})
            for d in range(1, sizes[n])
        ]

    def small_step(n):
        if n > 0:
            for copy in small_copies(n - 1):
                copy.wait_recv()
            total = s.small_held[n - 1]
            if n <= 3:
                for d in range(sizes[n - 1] - 1):
                    total = total + s.small_got[n - 1, d]
                s.small_held[n] = total
            else:
                both = total + s.small_got[3, 0]
                wide = width // lanes
                for c in range(2 * wide):
                    gains_out[c // wide : c // wide + 1, (c % wide) * lanes : (c % wide + 1) * lanes] = both[c : c + 1]
                bias_out[...] = total[2 * wide : 2 * wide + 1]
                for c in range(head_out.shape[1] // lanes):
                    head_out[:, c * lanes : (c + 1) * lanes] = total[2 * wide + 1 + c : 2 * wide + 2 + c]
        if n <= 3:
            for copy in small_copies(n):
                copy.start()

    most = s.wide_grads.shape[0]
    weight_loads = [
        pltpu.make_async_copy(down_weight.at[:most], s.wide_grads.at[:, :width], row_sem.at[6]),
        pltpu.make_async_copy(
            down_weight.at[most:], s.wide_grads.at[: hidden - most, width : 2 * width], row_sem.at[7]
        ),
    ]
    feed_rows = 2 * ROWS
    act_at, feed_at = hidden - most, hidden - most + feed_rows
    feed_ref = s.wide_grads.at[feed_at : feed_at + feed_rows, width : 2 * width]

    def feed_swap(n):
        return remote(feed_ref, feed_got.at[pl.ds(n * feed_rows, feed_rows)], swap_sems, 1 + steps + n, tp_peer)

    def feed_part(n):
        there = n < half // feed_rows
        start = (half if there else 0) + n % (half // feed_rows) * feed_rows
        load = pltpu.make_async_copy(
            act.at[start : start + feed_rows], s.wide_grads.at[act_at : act_at + feed_rows, width : width + hidden],
            feed_sem.at[n],
        )
        load.start()
        if n == 0:
            for copy in weight_loads:
                copy.wait()
        load.wait()
        left = s.wide_grads[act_at : act_at + feed_rows, width : width + hidden]
        part = dot(left[:, :most], s.wide_grads[:, :width])
        part = part + dot(left[:, most:], s.wide_grads[: hidden - most, width : 2 * width])
        if 0 < n <= half // feed_rows:
            feed_swap(n - 1).wait_send()
        s.wide_grads[feed_at : feed_at + feed_rows, width : 2 * width] = part.astype(BF)
        if there:
            feed_swap(n).start()

    def piece(n):
        if n == 0:
            for m in range(half // feed_rows):
                feed_swap(m).wait_recv()
        at = pl.ds(n * ROWS, ROWS)
        copies = [
            pltpu.make_async_copy(src.at[at], dst, piece_sem.at[n, i])
            for i, (src, dst) in enumerate(
                ((resid, s.wide.at[0]), (dresid, s.wide.at[1]), (tokens, s.narrow.at[0]), (feed_got, s.narrow.at[2]),
                 (dx_got, s.narrow.at[3]))
            )
        ]
        for copy in copies:
            copy.start()
        for copy in copies:
            copy.wait()
        lo = feed_at + n % 2 * ROWS
        feed = s.wide_grads[lo : lo + ROWS, width : 2 * width].astype(F32) + s.narrow[2].astype(F32)
        s.result[0] = (s.wide[0] + feed).astype(BF)
        dx = s.dx[mine(n)].astype(F32) + s.narrow[3].astype(F32)
        x = s.narrow[0].astype(F32)
        r = lax.rsqrt(jnp.mean(x * x, axis=-1, keepdims=True) + EPS)
        norm = x * r
        u = dx * s.norm_gain[...]
        s.result[1] = (s.wide[1] + r * (u - norm * jnp.mean(u * norm, axis=-1, keepdims=True))).astype(BF)
        ends = [
            pltpu.make_async_copy(s.result.at[i], out.at[at], piece_sem.at[n, 6 + i])
            for i, out in enumerate((block_out, tokens_out))
        ]
        for copy in ends:
            copy.start()
        for copy in ends:
            copy.wait()

    blocks = s.d_all.shape[1] // 128
    for n in range(-(-blocks // 4)):
        some = min(4, blocks - 4 * n)
        part = tn(s.xn[...], s.d_all[:, n * 512 : n * 512 + some * 128]).astype(BF)
        for c in range(some):
            s.mixer_units[4 * n + c] = part[:, c * 128 : (c + 1) * 128]
        small_step(n)
        tick()
    for copy in weight_loads:
        copy.start()
    dx_swap.wait()
    extras = [lambda n=n: feed_part(n) for n in range(half // feed_rows)]
    for n in range(half // feed_rows):
        extras.append(lambda n=n: feed_part(half // feed_rows + n))
        extras += [lambda m=m: piece(m) for m in (2 * n, 2 * n + 1)]
    step = 0
    while pending:
        tick()
        step += 1
        if step == 1:
            small_step(4)
        if extras and step % pieces == 0:
            extras.pop(0)()
    for extra in extras:
        extra()
    for copy in scans + [c for n in range(4) for c in small_copies(n)]:
        copy.wait_send()
    work.finish()


def back_call(rows, loaded, jobs, ticks, pieces):
    sizes = line_sizes(lax.axis_size("seq"))
    rounds = (sizes[0] * sizes[1] * sizes[2]).bit_length() - 1
    most = max(max(sizes) - 1, 1)
    half, width = rows[0].shape
    span, hidden = 2 * half, rows[2].shape[1]
    lanes, cols = loaded["wf"].shape[1], loaded["wq"].shape[1]
    small = (2 * width + lanes + cols) // lanes
    small = (small + -small % 8, lanes)
    mixer, ff = (3 * cols + lanes) // 128, 2 * hidden // 128
    out, down = (n * width // 128 // UNIT for n in (cols, hidden))
    shapes = [
        ((span, width), BF), ((span, width), BF), ((span, cols), BF), ((span, lanes), F32),
        ((span, 2 * hidden), BF), ((1, cols), F32), ((1, lanes), F32), ((1, width), F32), ((lanes, 2 * DH), F32),
        ((lanes, CH), F32), ((lanes, 2 * DH), F32), ((lanes, CH), F32), ((ff, UNIT, 128), BF),
        ((down, UNIT, 128), BF), ((mixer, UNIT, 128), BF), ((out, UNIT, 128), BF), ((1, width), F32), ((rounds, lanes, 2 * DH + 2 * CH), BF),
        ((rounds, lanes, 2 * DH + 2 * CH), BF), ((4, *small), F32), ((4, most, *small), F32), ((2, ROWS, width), F32),
        ((4, ROWS, width), BF), ((2, ROWS, width), BF),
    ]
    dma = pltpu.SemaphoreType.DMA
    scratch = [pltpu.VMEM(loaded[n].shape, loaded[n].dtype) for n in LOADED] + [pltpu.VMEM(*x) for x in shapes]
    scratch += [dma((len(LOADED),)), dma((8,)), dma((half // ROWS, 12)), dma((half // ROWS,))]
    scratch += [dma((rounds,))] * 2 + [dma((4, most))] * 2 + [dma((1 + half // ROWS + half // (2 * ROWS),))] * 2
    scratch += job_scratch(sizes, jobs, INSIDE)
    anywhere, vmem = pl.BlockSpec(memory_space=pl.ANY), pl.BlockSpec(memory_space=pltpu.VMEM)
    units = [(n, UNIT, 128) for n in (ff, down, mixer, out)]
    return pl.pallas_call(
        functools.partial(back_kernel, sizes, jobs, ticks, pieces),
        out_shape=[jax.ShapeDtypeStruct(x, F32) for x in ((2, width), (1, lanes), (1, cols))]
        + [jax.ShapeDtypeStruct((half, width), BF)] * 4 + [jax.ShapeDtypeStruct((half, width), F32)]
        + [jax.ShapeDtypeStruct(x, BF) for x in units],
        in_specs=[anywhere] * (len(rows) + len(LOADED)),
        out_specs=[vmem] * 3 + [anywhere] * 9,
        scratch_shapes=scratch,
        compiler_params=pltpu.CompilerParams(collective_id=0, has_side_effects=True, vmem_limit_bytes=63 * 1024 * 1024),
        name="back",
    )(*rows, *[loaded[n] for n in LOADED])


FRONT_LOADED = (
    "wq", "wk", "wv", "wf", "norm_gain", "bias", "code", "sums", "pairs", "gain", "wo", "feed_gain", "wg", "wu", "wd",
)
FRONT_SAVED = ("xn", "q", "k", "v", "dsq", "dsk", "gate", "weight", "dzf", "logits", "kvs", "mixed", "normed", "resid")
WIDE = 256


def silu_pair(raw):
    s = 1.0 / (1.0 + jnp.exp(-raw))
    return (raw * s).astype(BF), (s * (1.0 + raw * (1.0 - s))).astype(BF)


def project_rows(i, s):
    at = pl.ds(pl.multiple_of(i * WIDE, WIDE), WIDE)
    x = s.tokens[at].astype(F32)
    xn = (x * lax.rsqrt(jnp.mean(x * x, axis=-1, keepdims=True) + EPS) * s.norm_gain[...]).astype(BF)
    s.xn[at] = xn
    s.q[at], s.dsq[at] = silu_pair(dot(xn, s.wq[...]))
    s.k[at], s.dsk[at] = silu_pair(dot(xn, s.wk[...]))
    s.v[at] = dot(xn, s.wv[...]).astype(BF)
    z = dot(xn, s.wf[...]) + s.bias[...]
    code = s.code[at]
    valid, reset = code > 0.5, code > 1.5
    down = jnp.exp(-jnp.abs(z))
    gate = jnp.where(valid, (jnp.minimum(z, 0.0) - jnp.log(1.0 + down)) * (1.0 / NORMALIZER), 0.0)
    s.weight[at] = jnp.where(reset, 1.0, 1.0 - jnp.exp(gate))
    s.gate[at] = jnp.where(reset, RESET_LOG, gate)
    sig_neg = jnp.where(z > 0, down, 1.0) / (1.0 + down)
    s.dzf[at] = jnp.where(valid & (code < 1.5), sig_neg * (1.0 / NORMALIZER), 0.0)
    for c in range(WIDE // CH):
        part = chunk_rows(i * (WIDE // CH) + c)
        gate = s.gate[part]
        last = jnp.exp(dot(s.sums[CH : 2 * CH], split3(gate)))
        fade = fade_of(gate)
        s.total[...] = fade * s.total[...] + run_part((last * s.weight[part]).astype(BF), s.k[part], s.v[part])
        s.fade[...] = s.fade[...] * fade


def inner_chunk(c, s):
    at = chunk_rows(c)
    _, _, rows, cols, _ = decays(s.gate[at], s.weight[at], s.sums)
    q, k = s.q[at], s.k[at]
    s.logits[at] = through([nt(head(q, h), head(k, h)) for h in range(2)], rows, cols, s.pairs)


def mix_chunk(c, s):
    at = chunk_rows(c)
    q, k, v = s.q[at], s.k[at], s.v[at]
    gate, weight = s.gate[at], s.weight[at]
    first, last, rows, cols, _ = decays(gate, weight, s.sums)
    kv = s.enter[...]
    low = kv.astype(BF)
    s.kvs[c] = low
    outer = jnp.concatenate([nt(head(q, h), state(low, h)[:, :DH]) for h in range(2)], 1)
    logits = first * outer + s.logits[at]
    s.logits[at] = logits
    probs = softmax2(logits)
    reading = back_through([probs], rows, cols, s.pairs)
    spread = (probs * first).astype(BF)
    s.enter[...] = fade_of(gate) * kv + run_part((last * weight).astype(BF), k, v)
    code = s.code[at, :1]
    for h in range(2):
        mine = slice(h * DH, (h + 1) * DH)
        mixed = dot(slots(spread, h), state(low, h)[:, DH:]) + dot(reading[h].astype(BF), head(v, h))
        s.mixed[at, mine] = mixed
        r = lax.rsqrt(jnp.mean(mixed * mixed, axis=-1, keepdims=True) + EPS)
        s.normed[at, mine] = (mixed * jnp.where(code > 0.5, r, 0.0) * s.gain[:, mine]).astype(BF)


def feed_rows(n, s):
    at = pl.ds(n * WIDE, WIDE)
    hn, cot = s.hidden[at], s.cot[at]
    wide = s.wg.shape[1]
    slot = n % 2
    for c in range(0, wide, 512):
        some = slice(c, min(c + 512, wide))
        gate, up, dact = dot(hn, s.wg[:, some]), dot(hn, s.wu[:, some]), nt(cot, s.wd[some])
        sig = 1.0 / (1.0 + jnp.exp(-gate))
        soft = gate * sig
        s.act[slot, :, some] = (soft * up).astype(BF)
        s.dgate[slot, :, some] = (dact * up * sig * (1.0 + gate * (1.0 - sig))).astype(BF)
        s.dup[slot, :, some] = (dact * soft).astype(BF)
    s.dh[at] = (nt(s.dgate[slot], s.wg[...]) + nt(s.dup[slot], s.wu[...])).astype(BF)


def front_kernel(sizes, *refs):
    refs = list(refs)
    take = lambda n: [refs.pop(0) for _ in range(n)]
    tokens_own, cot_own = take(2)
    sources, saves = take(len(FRONT_LOADED)), take(len(FRONT_SAVED))
    hidden_out, cot_out, act_out, dgate_out, dup_out, dh_out, dh_got = take(7)
    s = Bag()
    for name in FRONT_LOADED + FRONT_SAVED:
        setattr(s, name, refs.pop(0))
    for name in ("tokens", "total", "fade", "enter", "reach", "sent", "got", "attn", "attn_got", "hidden", "cot", "act",
                 "dgate", "dup", "dh"):
        setattr(s, name, refs.pop(0))
    load_sem, save_sem, row_sem, part_sem = take(4)
    scan_sems, swap_sems = take(2), take(2)
    lines = Lines(sizes)
    half, width = tokens_own.shape
    count = 2 * half // CH
    tp_peer = {"tp": 1 - lines.half}
    own_rows = pl.ds(pl.multiple_of(lines.half * half, half), half)
    loads = [pltpu.make_async_copy(x, getattr(s, n), load_sem.at[i]) for i, (n, x) in enumerate(zip(FRONT_LOADED, sources))]
    late = loads[FRONT_LOADED.index("wo") :] + [pltpu.make_async_copy(cot_own, s.cot.at[pl.ds(0, half)], row_sem.at[1])]
    loads = loads[: FRONT_LOADED.index("wo")] + [pltpu.make_async_copy(tokens_own, s.tokens.at[own_rows], row_sem.at[0])]
    for copy in loads:
        copy.start()
    s.total[...] = jnp.zeros_like(s.total)
    s.fade[...] = jnp.ones_like(s.fade)
    lines.greet()
    tokens_swap = remote(tokens_own, s.tokens.at[own_rows], swap_sems, 0, tp_peer)
    tokens_swap.start()
    cot_swap = remote(cot_own, s.cot.at[pl.ds(half, half)], swap_sems, 1, tp_peer)
    cot_swap.start()
    for copy in late:
        copy.start()
    for copy in loads:
        copy.wait()
    tokens_swap.wait()

    def save(*names):
        for n in names:
            i = FRONT_SAVED.index(n)
            pltpu.make_async_copy(getattr(s, n), saves[i], save_sem.at[i]).start()

    lax.fori_loop(0, 2 * half // WIDE, lambda i, carry: (project_rows(i, s), carry)[1], 0)
    early = ("xn", "q", "k", "v", "dsq", "dsk", "gate", "weight", "dzf")
    save(*early)

    def between(n):
        if n < 4:
            for c in range(n * count // 4, (n + 1) * count // 4):
                inner_chunk(c, s)

    scans = scan_lines(lines, s.total, s.fade, s.enter, s.reach, s.sent, s.got, scan_sems, True, between)
    lax.fori_loop(0, count, lambda c, carry: (mix_chunk(c, s), carry)[1], 0)
    save("logits", "kvs", "mixed", "normed")

    for copy in late:
        copy.wait()
    steps = half // WIDE
    swaps = [
        remote(s.attn.at[pl.ds(n * WIDE, WIDE)], s.attn_got.at[pl.ds(n * WIDE, WIDE)], swap_sems, 2 + n, tp_peer)
        for n in range(steps)
    ]
    for n in range(2 * steps):
        side = (1 - lines.half) if n < steps else lines.half
        rows = pl.ds(pl.multiple_of(side * half + n % steps * WIDE, WIDE), WIDE)
        s.attn[n * WIDE : (n + 1) * WIDE] = dot(s.normed[rows], s.wo[...]).astype(BF)
        if n < steps:
            swaps[n].start()
    for n in range(steps):
        at = pl.ds(n * WIDE, WIDE)
        swaps[n].wait_recv()
        attn = s.attn[half + n * WIDE : half + (n + 1) * WIDE].astype(F32) + s.attn_got[at].astype(F32)
        x = s.tokens[pl.ds(pl.multiple_of(lines.half * half + n * WIDE, WIDE), WIDE)].astype(F32) + attn
        s.resid[at] = x
        r = lax.rsqrt(jnp.mean(x * x, axis=-1, keepdims=True) + EPS)
        s.hidden[at] = (x * r * s.feed_gain[...]).astype(BF)
        there = s.hidden.at[pl.ds(half + n * WIDE, WIDE)]
        swaps.append(remote(s.hidden.at[at], there, swap_sems, 2 + steps + n, tp_peer))
        swaps[-1].start()
    save("resid")
    cot_swap.wait()
    cot_save = pltpu.make_async_copy(s.cot, cot_out, row_sem.at[2])
    cot_save.start()

    outs = ((s.act, act_out), (s.dgate, dgate_out), (s.dup, dup_out))
    part = lambda n: [
        pltpu.make_async_copy(src.at[n % 2], dst.at[pl.ds(n * WIDE, WIDE)], part_sem.at[n, i])
        for i, (src, dst) in enumerate(outs)
    ]
    back = [
        remote(s.dh.at[pl.ds(half + n * WIDE, WIDE)], dh_got.at[pl.ds(n * WIDE, WIDE)], swap_sems, 2 + 2 * steps + n, tp_peer)
        for n in range(steps)
    ]
    busy = {}
    for n in [0] + list(range(steps, 2 * steps)) + list(range(1, steps)):
        if n % 2 in busy:
            for copy in busy[n % 2]:
                copy.wait()
        if n >= steps:
            swaps[n].wait_recv()
        feed_rows(n, s)
        busy[n % 2] = part(n)
        for copy in busy[n % 2]:
            copy.start()
        if n >= steps:
            back[n - steps].start()
    ends = [
        pltpu.make_async_copy(s.hidden, hidden_out, row_sem.at[3]),
        pltpu.make_async_copy(s.dh.at[pl.ds(0, half)], dh_out, row_sem.at[4]),
    ]
    for copy in ends:
        copy.start()
    for copy in ends + busy[0] + busy[1] + [cot_save]:
        copy.wait()
    for i, n in enumerate(FRONT_SAVED):
        pltpu.make_async_copy(getattr(s, n), saves[i], save_sem.at[i]).wait()
    for copy in back:
        copy.wait()
    for copy in scans + swaps:
        copy.wait_send()


def front_call(tokens, cot, loaded):
    sizes = line_sizes(lax.axis_size("seq"))
    rounds = (sizes[0] * sizes[1] * sizes[2]).bit_length() - 1
    half, width = tokens.shape
    span = 2 * half
    lanes, cols, hidden = (loaded[n].shape[1] for n in ("wf", "wq", "wg"))
    shapes = dict(
        xn=((span, width), BF), q=((span, cols), BF), k=((span, cols), BF), v=((span, cols), BF), dsq=((span, cols), BF),
        dsk=((span, cols), BF), gate=((span, lanes), F32), weight=((span, lanes), F32), dzf=((span, lanes), F32),
        logits=((span, lanes), F32), kvs=((span // CH, lanes, 2 * DH), BF), mixed=((span, cols), F32),
        normed=((span, cols), BF), resid=((half, width), F32),
    )
    others = [
        ((span, width), BF), ((lanes, 2 * DH), F32), ((lanes, CH), F32), ((lanes, 2 * DH), F32), ((lanes, CH), F32),
        ((rounds, lanes, 2 * DH + 2 * CH), BF), ((rounds, lanes, 2 * DH + 2 * CH), BF), ((span, width), BF), ((half, width), BF),
        ((span, width), BF), ((span, width), BF), ((2, WIDE, hidden), BF), ((2, WIDE, hidden), BF), ((2, WIDE, hidden), BF),
        ((span, width), BF),
    ]
    more = [((span, width), BF)] * 2 + [((span, hidden), BF)] * 3 + [((half, width), BF)] * 2
    dma = pltpu.SemaphoreType.DMA
    scratch = [pltpu.VMEM(loaded[n].shape, loaded[n].dtype) for n in FRONT_LOADED]
    scratch += [pltpu.VMEM(*shapes[n]) for n in FRONT_SAVED] + [pltpu.VMEM(*x) for x in others]
    scratch += [dma((len(FRONT_LOADED),)), dma((len(FRONT_SAVED),)), dma((5,)), dma((span // WIDE, 3))]
    scratch += [dma((rounds,))] * 2 + [dma((2 + 3 * (half // WIDE),))] * 2
    anywhere = pl.BlockSpec(memory_space=pl.ANY)
    outs = pl.pallas_call(
        functools.partial(front_kernel, sizes),
        out_shape=[jax.ShapeDtypeStruct(*x) for x in [shapes[n] for n in FRONT_SAVED] + more],
        in_specs=[anywhere] * (2 + len(FRONT_LOADED)),
        out_specs=[anywhere] * (len(FRONT_SAVED) + len(more)),
        scratch_shapes=scratch,
        compiler_params=pltpu.CompilerParams(collective_id=1, has_side_effects=True, vmem_limit_bytes=VMEM_LIMIT),
        name="front",
    )(tokens, cot, *[loaded[n] for n in FRONT_LOADED])
    return dict(zip(FRONT_SAVED, outs)), outs[len(FRONT_SAVED) :]


def widen_kernel(parts, *refs):
    for (which, blocks), out_ref in zip(parts, refs[-len(parts) :]):
        for c, block in enumerate(blocks):
            out_ref[:, c * 128 : (c + 1) * 128] = refs[which][block].astype(F32)


def widen(arrays, parts, steps):
    return pl.pallas_call(
        functools.partial(widen_kernel, parts),
        grid=(steps,),
        in_specs=[pl.BlockSpec((a.shape[0], a.shape[1] // steps, 128), lambda i: (0, i, 0)) for a in arrays],
        out_specs=[pl.BlockSpec((arrays[w].shape[1] // steps, len(b) * 128), lambda i: (i, 0)) for w, b in parts],
        out_shape=[jax.ShapeDtypeStruct((arrays[w].shape[1], len(b) * 128), F32) for w, b in parts],
        compiler_params=pltpu.CompilerParams(dimension_semantics=("arbitrary",), vmem_limit_bytes=VMEM_LIMIT),
        name="widen",
    )(*arrays)


X, Y, Z = 0, 1, 2
PIECES = 4
JOBS = (
    (2, 0, 1, (Y, X, Z)),
    (2, 1, 4, (Y, X, Z)),
    (3, 0, 4, (Y, X, Z)),
    (1, 0, 3, (Y, Z, X)),
    (0, 0, 4, (X, Y, Z)),
    (2, 5, 3, (X, Z, Y)),
    (1, 3, 4, (X, Y, Z)),
    (0, 4, 8, (Y, X, Z)),
    (2, 8, 3, (X, Y, Z)),
    (0, 12, 6, (X, Y, Z)),
    (2, 11, 2, (Z, Y, X)),
    (0, 18, 3, (X, Y, Z)),
    (1, 7, 4, (Y, X, Z)),
    (0, 21, 1, (Y, X, Z)),
)
TICKS = (
    (), ((3, 0),), ((6, 0),), ((12, 0),), (), (), (), ((3, 1),), (), (), ((6, 1),), (), ((12, 1), (3, 2), (4, 0),),
    ((6, 2), (7, 0),), ((12, 2), (3, 3), (9, 0),), ((6, 3), (4, 1), (3, 4),), ((12, 3), (7, 1), (2, 0), (11, 0),),
    ((4, 2), (9, 1), (6, 4),), (), (), ((3, 5),), ((2, 1), (7, 2),), ((12, 4),), (), ((4, 3), (9, 2), (11, 1),), (),
    ((1, 0),), ((2, 2), (6, 5),), ((7, 3),), ((12, 5),), ((5, 0),), ((3, 6),), ((4, 4),), ((8, 0),), ((11, 2),),
    ((6, 6),), ((9, 3),), ((0, 0),), ((10, 0),), ((1, 1),), ((2, 3),), ((5, 1),), ((8, 1),), ((12, 6),), ((7, 4),),
    ((1, 2),), ((11, 3),), ((4, 5),), ((0, 1),), ((13, 0),), ((8, 2),), ((9, 4),), ((7, 5),), ((13, 1),), ((10, 1),),
    ((9, 5),), ((4, 6),), ((0, 2),), ((13, 2),), ((2, 4),), ((5, 2),), ((1, 3),), ((9, 6),), ((7, 6),), ((11, 4),),
    ((10, 2),), ((5, 3),), ((2, 5),), ((8, 3),), ((10, 3),), ((0, 3),), ((11, 5),), ((13, 3),), ((5, 4),), ((10, 4),),
    ((1, 4),), ((11, 6),), ((8, 4),), ((0, 4),), ((2, 6),), ((13, 4),), ((10, 5),), ((1, 5),), ((0, 5),), ((8, 5),),
    ((13, 5),), ((5, 5),), ((8, 6),), ((1, 6),), ((0, 6),), ((10, 6),), ((13, 6),), ((5, 6),),
)


def token_code(lengths, positions):
    buckets = (lengths + BUCKET - 1) // BUCKET
    spans = buckets * BUCKET
    starts = jnp.cumsum(spans) - spans
    segment = jnp.sum((positions[:, None] >= starts[None, :]).astype(jnp.int32), axis=1) - 1
    picked = segment[:, None] == jnp.arange(lengths.shape[0], dtype=jnp.int32)[None, :]
    begin = jnp.sum(jnp.where(picked, starts[None, :], 0), axis=1)
    length = jnp.sum(jnp.where(picked, lengths[None, :], 0), axis=1)
    offset = positions - begin
    return jnp.where(offset == 0, 2.0, jnp.where(offset < length, 1.0, 0.0)).astype(F32)


def per_device(
    tokens, norm_gain, query_weight, key_weight, value_weight, forget_weight, forget_bias, head_gain,
    out_weight, feed_gain, gate_weight, up_weight, down_weight, lengths, cotangent,
):
    half, width = tokens.shape
    span = 2 * half
    cols = query_weight.shape[1]
    lanes = forget_weight.shape[1]
    sums, pairs, flipped, back = tables()
    sums, back = jnp.asarray(sums, BF), jnp.asarray(back, BF)
    pairs, flipped = jnp.asarray(pairs, BF), jnp.asarray(flipped, BF)

    positions = lax.axis_index("seq") * span + jnp.arange(span, dtype=jnp.int32)
    code = jnp.broadcast_to(token_code(lengths, positions)[:, None], (span, lanes))
    weights = dict(wq=query_weight, wk=key_weight, wv=value_weight, wf=forget_weight, wo=out_weight)
    shared = dict(code=code, sums=sums, pairs=pairs, gain=head_gain[None], norm_gain=norm_gain[None])
    wide = dict(wg=gate_weight, wu=up_weight, wd=down_weight, bias=forget_bias[None], feed_gain=feed_gain[None])
    saved, (hidden, cot, act, dgate, dup, dh_own, dh_got) = front_call(tokens, cotangent, dict(weights, **shared, **wide))
    resid = saved["resid"]
    loaded = dict(weights, **shared, flipped=flipped, back=back, feed_gain=feed_gain[None])
    for name in ("q", "k", "v", "dsq", "dsk", "gate", "weight", "dzf", "logits", "kvs", "mixed", "normed"):
        loaded[name] = saved[name]
    rows = (dh_own, dh_got, act, cot, hidden, dgate, dup, down_weight, resid, tokens, saved["xn"])
    gains, bias_sum, head_sum, block_out, tokens_grad, _, _, _, *sums = back_call(rows, loaded, JOBS, TICKS, PIECES)
    ff_sum, down_sum, mixer_sum, out_sum = sums
    blocks, ff_blocks, wide = cols // 128, gate_weight.shape[1] // 128, tuple(range(width // 128))
    which = lambda up: tuple(4 * (c // 2) + 2 * up + c % 2 - (up if c == ff_blocks - 1 else 0) for c in range(ff_blocks))
    parts = [(0, tuple(range(i * blocks, (i + 1) * blocks))) for i in range(3)] + [(0, (3 * blocks,)), (1, wide)]
    parts += [(2, which(0)), (2, which(1)), (3, wide)]
    arrays = [mixer_sum, out_sum.reshape(-1, cols, 128), ff_sum, down_sum.reshape(-1, down_weight.shape[0], 128)]
    query_sum, key_sum, value_sum, forget_sum, out_grad, gate_grad, up_grad, down_grad = widen(arrays, parts, 8)
    return (
        block_out, tokens_grad, gains[0], query_sum, key_sum, value_sum, forget_sum, bias_sum[0], head_sum[0], out_grad,
        gains[1], gate_grad, up_grad, down_grad,
    )


def solution(mesh):
    rows, by_col, by_row = P(("seq", "tp"), None), P(None, "tp"), P("tp", None)
    return jax.shard_map(
        per_device,
        mesh=mesh,
        in_specs=(
            rows, P(), by_col, by_col, by_col, by_col, P("tp"), P("tp"), by_row, P(), by_col, by_col, by_row, P(), rows,
        ),
        out_specs=(
            rows, rows, P(), by_col, by_col, by_col, by_col, P("tp"), P("tp"), by_row, P(), by_col, by_col, by_row,
        ),
        check_vma=False,
    )
```

profile of v0, /device:TPU:0, one launch (start us, length us, event | category | flops | bytes accessed | tf_op | source)
XLA Modules:
  0.0 340.4 jit_solution(3874356205698141299)
XLA Ops:
  0.6 0.7 fusion.2
  1.3 0.2 reduce-window.9
  1.5 0.7 bitcast_subtract_fusion
  2.2 0.1 convert_reduce_fusion
  2.3 0.8 select_reduce_fusion.1
  3.0 1.0 broadcast_in_dim.60.refs_8_.refs_13_
  4.0 76.6 %front.1 = (bf16[1024,1024]{1,0:T(8,128)(2,1)}, bf16[1024,512]{1,0:T(8,128)(2,1)}, bf16[1024,512]{1,0:T(8,128)(2,1)}, bf16[1024,512]{1,0:T(8,128)(2,1)}, bf16[10...) custom-call(bf16[512,1024]{1,0:T(8,128)(2,1)} %refs_9_.2, ...), custom_call_target="tpu_custom_call" | custom-call | tf_op jit(solution)/shard_map/front/pallas_call | solution.py:1024
  80.6 240.7 %back.1 = (f32[2,1024]{1,0:T(2,128)}, f32[1,128]{1,0:T(1,128)}, f32[1,512]{1,0:T(1,128)}, bf16[512,1024]{1,0:T(8,128)(2,1)}, bf16[512,1024]{1,0:T(8,128)(2,1)}, ...) custom-call(bf16[512,1024]{1,0:T(8,128)(2,1)} %get-tuple-element.52., ...), custom_call_target="tpu_custom_call" | custom-call | tf_op jit(solution)/shard_map/back/pallas_call | solution.py:779
  321.3 1.4 fusion.1
  322.7 0.0 copy-start.1
  322.7 0.0 copy-start
  322.7 14.5 %widen.1 = (f32[1024,512]{1,0:T(8,128)}, f32[1024,512]{1,0:T(8,128)}, f32[1024,512]{1,0:T(8,128)}, f32[1024,128]{1,0:T(8,128)}, f32[512,1024]{1,0:T(8,128)}, /*i...) custom-call(bf16[13,1024,128]{2,1,0:T(8,128)(2,1)} %get-tuple-element.76.refs_0_, ...), custom_call_target="tpu_custom_call" | custom-call | tf_op jit(solution)/shard_map/widen/pallas_call | solution.py:1043
  337.2 0.0 copy-start.3
  337.2 0.0 copy-start.2
  337.2 0.0 copy-done.1
  337.2 1.0 copy.37
  338.2 0.0 copy-done
  338.2 1.0 copy.38
  339.1 0.0 copy-done.3
  339.1 0.5 copy.39
  339.6 0.0 copy-done.2
  339.6 0.6 copy.40
  (3 shorter events, 0.0 us)
Async XLA Ops:
  322.7 14.5 %copy-start.1 = (bf16[512,1024]{1,0:T(8,128)(2,1)S(1)}, bf16[512,1024]{1,0:T(8,128)(2,1)}, u32[]{:S(2)}) copy-start(bf16[512,1024]{1,0:T(8,128)(2,1)} %get-tuple-element.108) | copy-start | bytes 3145732
  322.7 15.5 %copy-start = (bf16[512,1024]{1,0:T(8,128)(2,1)S(1)}, bf16[512,1024]{1,0:T(8,128)(2,1)}, u32[]{:S(2)}) copy-start(bf16[512,1024]{1,0:T(8,128)(2,1)} %get-tuple-element.109) | copy-start | bytes 3145732
  337.2 2.0 copy-start.3
  337.2 2.5 copy-start.2
where the time goes:
time: 346 us; the launch traced here: 340 us
  Pallas kernels  332 us (96%)
  local copies, waits for them, and re-layouts  5.42 us (2%)
    pallas_call x1, Pallas kernels, back_call(): pl.pallas_call(functools.partial(back_kernel, sizes, jobs, ticks, pieces)...  241 us
    pallas_call x1, Pallas kernels, front_call(): pl.pallas_call(functools.partial(front_kernel, sizes), out_shape=[jax.Sha...  76.6 us
    pallas_call x1, Pallas kernels, widen(): pl.pallas_call(functools.partial(widen_kernel, parts), grid=(steps,), in_...  14.5 us

commit v1 on v0

--- a/solution.py
+++ b/solution.py
@@ -203,6 +203,9 @@
     return scratch + [pltpu.SemaphoreType.DMA((len(jobs), 6, most))] * 2 + [pltpu.SemaphoreType.DMA((len(jobs), 2))]
 
 
+TAIL = 16
+
+
 class Jobs:
     def __init__(self, lines, jobs, ins, outs, inside, scratch):
         self.lines, self.jobs, self.ins, self.outs, self.inside = lines, jobs, ins, outs, inside
@@ -297,8 +300,9 @@
 
 
 def scan_lines(lines, total_ref, fade_ref, enter_ref, reach_ref, sent_ref, got_ref, sems, earlier, between):
-    width = total_ref.shape[1]
     enter_ref[...] = jnp.zeros_like(enter_ref)
+    for bit in range(sent_ref.shape[0]):
+        sent_ref[bit, total_ref.shape[0] :] = jnp.zeros_like(sent_ref[bit, total_ref.shape[0] :])
     reach_ref[...] = jnp.ones_like(reach_ref)
     count = lines.sizes[0] * lines.sizes[1] * lines.sizes[2]
     rounds = count.bit_length() - 1
@@ -308,17 +312,20 @@
         partner = lines.index + (1 - 2 * side[bit]) * (1 << bit)
         return remote(sent_ref.at[bit], got_ref.at[bit], sems, bit, {"seq": partner})
 
+    lanes = total_ref.shape[0]
     for bit in range(rounds):
         fade = fade_ref[...]
-        high = fade.astype(BF)
-        sent_ref[bit, :, :width] = total_ref[...].astype(BF)
-        sent_ref[bit, :, width : width + CH] = high
-        sent_ref[bit, :, width + CH :] = (fade - high.astype(F32)).astype(BF)
+        flat = fade.T[:1]
+        high = flat.astype(BF).astype(F32)
+        sent_ref[bit, :lanes] = total_ref[...].astype(BF)
+        row = lax.broadcasted_iota(jnp.int32, (TAIL, lanes), 0)
+        sent_ref[bit, lanes:, :lanes] = jnp.where(row == 0, high, flat - high).astype(BF)
         copy(bit).start()
         between(bit)
         copy(bit).wait_recv()
-        part = got_ref[bit, :, :width].astype(F32)
-        part_fade = got_ref[bit, :, width : width + CH].astype(F32) + got_ref[bit, :, width + CH :].astype(F32)
+        part = got_ref[bit, :lanes].astype(F32)
+        flat = got_ref[bit, lanes:, :lanes].astype(F32)
+        part_fade = jnp.broadcast_to(flat[:1] + flat[1:2], fade.shape).T
         behind = side[bit] == (1 if earlier else 0)
         enter, reach, total = enter_ref[...], reach_ref[...], total_ref[...]
         enter_ref[...] = jnp.where(behind, reach[:, :1] * part + enter, enter)
@@ -449,7 +456,7 @@
     take = lambda n: [refs.pop(0) for _ in range(n)]
     dh_own, dh_got, act, cot, hn, dgate, dup, down_weight, resid, tokens, xn = take(11)
     sources = take(len(LOADED))
-    gains_out, bias_out, head_out, block_out, tokens_out, feed_got, dx_got, dresid, *outs = take(12)
+    norm_out, feed_out, bias_out, head_out, block_out, tokens_out, feed_got, dx_got, dresid, *outs = take(13)
     s = Bag()
     for name in LOADED:
         setattr(s, name, refs.pop(0))
@@ -479,7 +486,7 @@
         pltpu.make_async_copy(dgate, s.dgate, row_sem.at[3]),
         pltpu.make_async_copy(dup, s.dup, row_sem.at[4]),
     ]
-    for copy in early + loads + late[:1]:
+    for copy in early + loads[::-1] + late[:1]:
         copy.start()
     for ref in (s.gain_grad, s.bias_grad, s.norm_grad, s.feed_part, s.dkv):
         ref[...] = jnp.zeros_like(ref)
@@ -512,7 +519,8 @@
 
         lax.fori_loop(0, count, one, 0)
 
-    for copy in early:
+    feed_gain = loads.pop(LOADED.index("feed_gain"))
+    for copy in early + [feed_gain]:
         copy.wait()
 
     def down_part(n):
@@ -561,12 +569,10 @@
     for n in range(2):
         for copy in row_loads(n):
             copy.start()
-    for copy in loads:
-        copy.wait()
     for n in range(steps):
+        down_part(n)
         row_grads(n)
         da_swaps[n].start()
-        down_part(n)
         dresid_save(n).wait()
         if n + 2 < steps:
             for copy in row_loads(n + 2):
@@ -574,6 +580,8 @@
         tick()
     for copy in late[1:]:
         copy.start()
+    for copy in loads:
+        copy.wait()
     for copy in da_swaps:
         copy.wait_recv()
     loop(lambda i: score_chunk(i, s))
@@ -643,7 +651,7 @@
                 both = total + s.small_got[3, 0]
                 wide = width // lanes
                 for c in range(2 * wide):
-                    gains_out[c // wide : c // wide + 1, (c % wide) * lanes : (c % wide + 1) * lanes] = both[c : c + 1]
+                    (norm_out, feed_out)[c // wide][:, (c % wide) * lanes : (c % wide + 1) * lanes] = both[c : c + 1]
                 bias_out[...] = total[2 * wide : 2 * wide + 1]
                 for c in range(head_out.shape[1] // lanes):
                     head_out[:, c * lanes : (c + 1) * lanes] = total[2 * wide + 1 + c : 2 * wide + 2 + c]
@@ -765,8 +773,8 @@
         ((span, width), BF), ((span, width), BF), ((span, cols), BF), ((span, lanes), F32),
         ((span, 2 * hidden), BF), ((1, cols), F32), ((1, lanes), F32), ((1, width), F32), ((lanes, 2 * DH), F32),
         ((lanes, CH), F32), ((lanes, 2 * DH), F32), ((lanes, CH), F32), ((ff, UNIT, 128), BF),
-        ((down, UNIT, 128), BF), ((mixer, UNIT, 128), BF), ((out, UNIT, 128), BF), ((1, width), F32), ((rounds, lanes, 2 * DH + 2 * CH), BF),
-        ((rounds, lanes, 2 * DH + 2 * CH), BF), ((4, *small), F32), ((4, most, *small), F32), ((2, ROWS, width), F32),
+        ((down, UNIT, 128), BF), ((mixer, UNIT, 128), BF), ((out, UNIT, 128), BF), ((1, width), F32), ((rounds, lanes + TAIL, 2 * DH), BF),
+        ((rounds, lanes + TAIL, 2 * DH), BF), ((4, *small), F32), ((4, most, *small), F32), ((2, ROWS, width), F32),
         ((4, ROWS, width), BF), ((2, ROWS, width), BF),
     ]
     dma = pltpu.SemaphoreType.DMA
@@ -778,11 +786,11 @@
     units = [(n, UNIT, 128) for n in (ff, down, mixer, out)]
     return pl.pallas_call(
         functools.partial(back_kernel, sizes, jobs, ticks, pieces),
-        out_shape=[jax.ShapeDtypeStruct(x, F32) for x in ((2, width), (1, lanes), (1, cols))]
+        out_shape=[jax.ShapeDtypeStruct(x, F32) for x in ((1, width), (1, width), (1, lanes), (1, cols))]
         + [jax.ShapeDtypeStruct((half, width), BF)] * 4 + [jax.ShapeDtypeStruct((half, width), F32)]
         + [jax.ShapeDtypeStruct(x, BF) for x in units],
         in_specs=[anywhere] * (len(rows) + len(LOADED)),
-        out_specs=[vmem] * 3 + [anywhere] * 9,
+        out_specs=[vmem] * 4 + [anywhere] * 9,
         scratch_shapes=scratch,
         compiler_params=pltpu.CompilerParams(collective_id=0, has_side_effects=True, vmem_limit_bytes=63 * 1024 * 1024),
         name="back",
@@ -790,15 +798,26 @@
 
 
 FRONT_LOADED = (
-    "wq", "wk", "wv", "wf", "norm_gain", "bias", "code", "sums", "pairs", "gain", "wo", "feed_gain", "wg", "wu", "wd",
+    "wq", "wk", "wv", "wf", "norm_gain", "bias", "sums", "pairs", "gain", "wo", "feed_gain", "wg", "wu", "wd",
 )
-FRONT_SAVED = ("xn", "q", "k", "v", "dsq", "dsk", "gate", "weight", "dzf", "logits", "kvs", "mixed", "normed", "resid")
+FRONT_SAVED = ("code", "xn", "q", "k", "v", "dsq", "dsk", "gate", "weight", "dzf", "logits", "kvs", "mixed", "normed", "resid")
 WIDE = 256
 
 
 def silu_pair(raw):
     s = 1.0 / (1.0 + jnp.exp(-raw))
     return (raw * s).astype(BF), (s * (1.0 + raw * (1.0 - s))).astype(BF)
+
+
+def token_code(lengths, positions):
+    start, code = 0, jnp.zeros(positions.shape, F32)
+    for i in range(lengths.shape[0]):
+        length = lengths[i]
+        stop = start + (length + BUCKET - 1) // BUCKET * BUCKET
+        mark = jnp.where(positions == start, 2.0, jnp.where(positions < start + length, 1.0, 0.0))
+        code = jnp.where((positions >= start) & (positions < stop), mark, code)
+        start = stop
+    return code
 
 
 def project_rows(i, s):
@@ -810,7 +829,8 @@
     s.k[at], s.dsk[at] = silu_pair(dot(xn, s.wk[...]))
     s.v[at] = dot(xn, s.wv[...]).astype(BF)
     z = dot(xn, s.wf[...]) + s.bias[...]
-    code = s.code[at]
+    code = token_code(s.lengths, lax.broadcasted_iota(jnp.int32, z.shape, 0) + s.first_row + i * WIDE)
+    s.code[at] = code
     valid, reset = code > 0.5, code > 1.5
     down = jnp.exp(-jnp.abs(z))
     gate = jnp.where(valid, (jnp.minimum(z, 0.0) - jnp.log(1.0 + down)) * (1.0 / NORMALIZER), 0.0)
@@ -818,27 +838,30 @@
     s.gate[at] = jnp.where(reset, RESET_LOG, gate)
     sig_neg = jnp.where(z > 0, down, 1.0) / (1.0 + down)
     s.dzf[at] = jnp.where(valid & (code < 1.5), sig_neg * (1.0 / NORMALIZER), 0.0)
-    for c in range(WIDE // CH):
-        part = chunk_rows(i * (WIDE // CH) + c)
+    for n in range(WIDE // CH):
+        c = i * (WIDE // CH) + n
+        part = chunk_rows(c)
         gate = s.gate[part]
         last = jnp.exp(dot(s.sums[CH : 2 * CH], split3(gate)))
-        fade = fade_of(gate)
-        s.total[...] = fade * s.total[...] + run_part((last * s.weight[part]).astype(BF), s.k[part], s.v[part])
-        s.fade[...] = s.fade[...] * fade
+        s.adds[c] = run_part((last * s.weight[part]).astype(BF), s.k[part], s.v[part])
+        s.fades[c] = jnp.broadcast_to(fade_of(gate), (gate.shape[1], CH))
 
 
 def inner_chunk(c, s):
     at = chunk_rows(c)
-    _, _, rows, cols, _ = decays(s.gate[at], s.weight[at], s.sums)
+    first, _, rows, cols, _ = decays(s.gate[at], s.weight[at], s.sums)
+    s.first[at] = first
+    for i in range(len(rows)):
+        s.rows[i, at], s.cols[i, at] = rows[i], cols[i].astype(BF)
     q, k = s.q[at], s.k[at]
     s.logits[at] = through([nt(head(q, h), head(k, h)) for h in range(2)], rows, cols, s.pairs)
 
 
 def mix_chunk(c, s):
     at = chunk_rows(c)
-    q, k, v = s.q[at], s.k[at], s.v[at]
-    gate, weight = s.gate[at], s.weight[at]
-    first, last, rows, cols, _ = decays(gate, weight, s.sums)
+    q, v = s.q[at], s.v[at]
+    first = s.first[at]
+    rows, cols = ([ref[i, at] for i in range(len(HALVES) + 1)] for ref in (s.rows, s.cols))
     kv = s.enter[...]
     low = kv.astype(BF)
     s.kvs[c] = low
@@ -848,7 +871,7 @@
     probs = softmax2(logits)
     reading = back_through([probs], rows, cols, s.pairs)
     spread = (probs * first).astype(BF)
-    s.enter[...] = fade_of(gate) * kv + run_part((last * weight).astype(BF), k, v)
+    s.enter[...] = s.fades[c, :, :1] * kv + s.adds[c]
     code = s.code[at, :1]
     for h in range(2):
         mine = slice(h * DH, (h + 1) * DH)
@@ -877,15 +900,17 @@
 def front_kernel(sizes, *refs):
     refs = list(refs)
     take = lambda n: [refs.pop(0) for _ in range(n)]
-    tokens_own, cot_own = take(2)
+    lengths, tokens_own, cot_own = take(3)
     sources, saves = take(len(FRONT_LOADED)), take(len(FRONT_SAVED))
     hidden_out, cot_out, act_out, dgate_out, dup_out, dh_out, dh_got = take(7)
     s = Bag()
     for name in FRONT_LOADED + FRONT_SAVED:
         setattr(s, name, refs.pop(0))
     for name in ("tokens", "total", "fade", "enter", "reach", "sent", "got", "attn", "attn_got", "hidden", "cot", "act",
-                 "dgate", "dup", "dh"):
+                 "dgate", "dup", "first", "rows", "cols", "adds", "fades"):
         setattr(s, name, refs.pop(0))
+    s.lengths = lengths
+    s.dh = s.xn
     load_sem, save_sem, row_sem, part_sem = take(4)
     scan_sems, swap_sems = take(2), take(2)
     lines = Lines(sizes)
@@ -898,8 +923,7 @@
     loads = loads[: FRONT_LOADED.index("wo")] + [pltpu.make_async_copy(tokens_own, s.tokens.at[own_rows], row_sem.at[0])]
     for copy in loads:
         copy.start()
-    s.total[...] = jnp.zeros_like(s.total)
-    s.fade[...] = jnp.ones_like(s.fade)
+    s.first_row = lines.index * (2 * half)
     lines.greet()
     tokens_swap = remote(tokens_own, s.tokens.at[own_rows], swap_sems, 0, tp_peer)
     tokens_swap.start()
@@ -909,15 +933,22 @@
         copy.start()
     for copy in loads:
         copy.wait()
-    tokens_swap.wait()
 
     def save(*names):
         for n in names:
             i = FRONT_SAVED.index(n)
             pltpu.make_async_copy(getattr(s, n), saves[i], save_sem.at[i]).start()
 
-    lax.fori_loop(0, 2 * half // WIDE, lambda i, carry: (project_rows(i, s), carry)[1], 0)
-    early = ("xn", "q", "k", "v", "dsq", "dsk", "gate", "weight", "dzf")
+    for side in (lines.half, 1 - lines.half):
+        lax.fori_loop(0, half // WIDE, lambda i, carry: (project_rows(side * (half // WIDE) + i, s), carry)[1], 0)
+        if side is lines.half:
+            tokens_swap.wait()
+    total, fade = s.adds[0], s.fades[0]
+    for c in range(1, count):
+        total = s.fades[c, :, :1] * total + s.adds[c]
+        fade = fade * s.fades[c]
+    s.total[...], s.fade[...] = total, fade
+    early = ("code", "xn", "q", "k", "v", "dsq", "dsk", "gate", "weight", "dzf")
     save(*early)
 
     def between(n):
@@ -968,6 +999,8 @@
         for n in range(steps)
     ]
     busy = {}
+    at_xn = FRONT_SAVED.index("xn")
+    pltpu.make_async_copy(s.xn, saves[at_xn], save_sem.at[at_xn]).wait()
     for n in [0] + list(range(steps, 2 * steps)) + list(range(1, steps)):
         if n % 2 in busy:
             for copy in busy[n % 2]:
@@ -989,20 +1022,23 @@
     for copy in ends + busy[0] + busy[1] + [cot_save]:
         copy.wait()
     for i, n in enumerate(FRONT_SAVED):
-        pltpu.make_async_copy(getattr(s, n), saves[i], save_sem.at[i]).wait()
+        if i != at_xn:
+            pltpu.make_async_copy(getattr(s, n), saves[i], save_sem.at[i]).wait()
     for copy in back:
         copy.wait()
     for copy in scans + swaps:
         copy.wait_send()
 
 
-def front_call(tokens, cot, loaded):
+def front_call(lengths, tokens, cot, loaded):
     sizes = line_sizes(lax.axis_size("seq"))
     rounds = (sizes[0] * sizes[1] * sizes[2]).bit_length() - 1
     half, width = tokens.shape
     span = 2 * half
     lanes, cols, hidden = (loaded[n].shape[1] for n in ("wf", "wq", "wg"))
+    levels = len(HALVES) + 1
     shapes = dict(
+        code=((span, lanes), F32),
         xn=((span, width), BF), q=((span, cols), BF), k=((span, cols), BF), v=((span, cols), BF), dsq=((span, cols), BF),
         dsk=((span, cols), BF), gate=((span, lanes), F32), weight=((span, lanes), F32), dzf=((span, lanes), F32),
         logits=((span, lanes), F32), kvs=((span // CH, lanes, 2 * DH), BF), mixed=((span, cols), F32),
@@ -1010,9 +1046,10 @@
     )
     others = [
         ((span, width), BF), ((lanes, 2 * DH), F32), ((lanes, CH), F32), ((lanes, 2 * DH), F32), ((lanes, CH), F32),
-        ((rounds, lanes, 2 * DH + 2 * CH), BF), ((rounds, lanes, 2 * DH + 2 * CH), BF), ((span, width), BF), ((half, width), BF),
+        ((rounds, lanes + TAIL, 2 * DH), BF), ((rounds, lanes + TAIL, 2 * DH), BF), ((span, width), BF), ((half, width), BF),
         ((span, width), BF), ((span, width), BF), ((2, WIDE, hidden), BF), ((2, WIDE, hidden), BF), ((2, WIDE, hidden), BF),
-        ((span, width), BF),
+        ((span, lanes), F32), ((levels, span, lanes), F32), ((levels, span, lanes), BF),
+        ((span // CH, lanes, 2 * DH), F32), ((span // CH, lanes, CH), F32),
     ]
     more = [((span, width), BF)] * 2 + [((span, hidden), BF)] * 3 + [((half, width), BF)] * 2
     dma = pltpu.SemaphoreType.DMA
@@ -1024,12 +1061,324 @@
     outs = pl.pallas_call(
         functools.partial(front_kernel, sizes),
         out_shape=[jax.ShapeDtypeStruct(*x) for x in [shapes[n] for n in FRONT_SAVED] + more],
-        in_specs=[anywhere] * (2 + len(FRONT_LOADED)),
+        in_specs=[pl.BlockSpec(memory_space=pltpu.SMEM)] + [anywhere] * (2 + len(FRONT_LOADED)),
         out_specs=[anywhere] * (len(FRONT_SAVED) + len(more)),
         scratch_shapes=scratch,
-        compiler_params=pltpu.CompilerParams(collective_id=1, has_side_effects=True, vmem_limit_bytes=VMEM_LIMIT),
+        compiler_params=pltpu.CompilerParams(collective_id=1, has_side_effects=True, vmem_limit_bytes=63 * 1024 * 1024),
         name="front",
-    )(tokens, cot, *[loaded[n] for n in FRONT_LOADED])
+    )(lengths, tokens, cot, *[loaded[n] for n in FRONT_LOADED])
+    return dict(zip(FRONT_SAVED, outs)), outs[len(FRONT_SAVED) :]
+
+
+def widen_kernel(parts, *refs):
+    for (which, blocks), out_ref in zip(parts, refs[-len(parts) :]):
+        for c, block in enumerate(blocks):
+            out_ref[:, c * 128 : (c + 1) * 128] = refs[which][block].astype(F32)
+
+
+def widen(arrays, parts, steps):
+    return pl.pallas_call(
+        functools.partial(widen_kernel, parts),
+        grid=(steps,),
+        in_specs=[pl.BlockSpec((a.shape[0], a.shape[1] // steps, 128), lambda i: (0, i, 0)) for a in arrays],
+        out_specs=[pl.BlockSpec((arrays[w].shape[1] // steps, len(b) * 128), lambda i: (i, 0)) for w, b in parts],
+        out_shape=[jax.ShapeDtypeStruct((arrays[w].shape[1], len(b) * 128), F32) for w, b in parts],
+        compiler_params=pltpu.CompilerParams(dimension_semantics=("arbitrary",), vmem_limit_bytes=VMEM_LIMIT),
+        name="widen",
+    )(*arrays)
+
+
+X, Y, Z = 0, 1, 2
+PIECES = 4
+JOBS = (
+    (2, 0, 5, (X, Y, Z)),
+    (1, 0, 4, (Y, X, Z)),
+    (2, 5, 2, (X, Y, Z)),
+    (1, 4, 1, (X, Y, Z)),
+    (3, 0, 1, (Z, Y, X)),
+    (3, 1, 3, (Y, Z, X)),
+    (0, 0, 6, (X, Y, Z)),
+    (0, 6, 5, (Y, X, Z)),
+    (1, 5, 2, (Y, Z, X)),
+    (0, 11, 8, (X, Y, Z)),
+    (2, 7, 3, (Y, Z, X)),
+    (0, 19, 3, (Y, X, Z)),
+    (2, 10, 3, (X, Y, Z)),
+    (1, 7, 4, (X, Y, Z)),
+)
+TICKS = (
+    (), ((1, 0), (3, 0),), ((8, 0),), ((13, 0),), ((3, 1),), (), (), (), ((1, 1),), (), (), ((13, 1), (8, 1),),
+    ((3, 2), (1, 2), (6, 0),), ((13, 2), (8, 2), (3, 3), (7, 0),), ((1, 3), (9, 0),),
+    ((13, 3), (3, 4), (6, 1), (8, 3), (11, 0),), ((7, 1), (1, 4), (3, 5), (6, 2),), ((13, 4),), (),
+    ((9, 1), (8, 4), (11, 1),), ((6, 3),), ((13, 5), (7, 2),), ((8, 5),), ((1, 5),), ((3, 6),), ((9, 2),),
+    ((6, 4), (11, 2), (2, 0),), ((10, 0),), ((12, 0),), ((8, 6),), ((7, 3),), ((0, 0),), ((13, 6),), ((1, 6),),
+    ((2, 1),), ((9, 3),), ((11, 3),), ((6, 5),), ((12, 1),), ((7, 4),), ((10, 1),), ((5, 0),), ((2, 2),), ((12, 2),),
+    ((0, 1),), ((9, 4),), ((11, 4),), ((5, 1),), ((4, 0),), ((10, 2),), ((0, 2),), ((2, 3),), ((6, 6),), ((12, 3),),
+    ((7, 5),), ((9, 5),), ((11, 5),), ((5, 2),), ((10, 3),), ((4, 1),), ((7, 6),), ((0, 3),), ((2, 4),), ((12, 4),),
+    ((11, 6),), ((4, 2),), ((9, 6),), ((2, 5),), ((5, 3),), ((10, 4),), ((4, 3),), ((0, 4),), ((12, 5),), ((2, 6),),
+    ((5, 4),), ((4, 4),), ((10, 5),), ((0, 5),), ((4, 5),), ((12, 6),), ((5, 5),), ((10, 6),), ((4, 6),), ((5, 6),),
+    ((0, 6),),
+)
+
+
+def token_code(lengths, positions):
+    start, code = 0, jnp.zeros(positions.shape, F32)
+    for i in range(lengths.shape[0]):
+        length = lengths[i]
+        stop = start + (length + BUCKET - 1) // BUCKET * BUCKET
+        mark = jnp.where(positions == start, 2.0, jnp.where(positions < start + length, 1.0, 0.0))
+        code = jnp.where((positions >= start) & (positions < stop), mark, code)
+        start = stop
+    return code
+
+
+def project_rows(i, s):
+    at = pl.ds(pl.multiple_of(i * WIDE, WIDE), WIDE)
+    x = s.tokens[at].astype(F32)
+    xn = (x * lax.rsqrt(jnp.mean(x * x, axis=-1, keepdims=True) + EPS) * s.norm_gain[...]).astype(BF)
+    s.xn[at] = xn
+    s.q[at], s.dsq[at] = silu_pair(dot(xn, s.wq[...]))
+    s.k[at], s.dsk[at] = silu_pair(dot(xn, s.wk[...]))
+    s.v[at] = dot(xn, s.wv[...]).astype(BF)
+    z = dot(xn, s.wf[...]) + s.bias[...]
+    code = token_code(s.lengths, lax.broadcasted_iota(jnp.int32, z.shape, 0) + s.first_row + i * WIDE)
+    s.code[at] = code
+    valid, reset = code > 0.5, code > 1.5
+    down = jnp.exp(-jnp.abs(z))
+    gate = jnp.where(valid, (jnp.minimum(z, 0.0) - jnp.log(1.0 + down)) * (1.0 / NORMALIZER), 0.0)
+    s.weight[at] = jnp.where(reset, 1.0, 1.0 - jnp.exp(gate))
+    s.gate[at] = jnp.where(reset, RESET_LOG, gate)
+    sig_neg = jnp.where(z > 0, down, 1.0) / (1.0 + down)
+    s.dzf[at] = jnp.where(valid & (code < 1.5), sig_neg * (1.0 / NORMALIZER), 0.0)
+    for n in range(WIDE // CH):
+        c = i * (WIDE // CH) + n
+        part = chunk_rows(c)
+        gate = s.gate[part]
+        last = jnp.exp(dot(s.sums[CH : 2 * CH], split3(gate)))
+        s.adds[c] = run_part((last * s.weight[part]).astype(BF), s.k[part], s.v[part])
+        s.fades[c] = jnp.broadcast_to(fade_of(gate), (gate.shape[1], CH))
+
+
+def inner_chunk(c, s):
+    at = chunk_rows(c)
+    first, _, rows, cols, _ = decays(s.gate[at], s.weight[at], s.sums)
+    s.first[at] = first
+    for i in range(len(rows)):
+        s.rows[i, at], s.cols[i, at] = rows[i], cols[i].astype(BF)
+    q, k = s.q[at], s.k[at]
+    s.logits[at] = through([nt(head(q, h), head(k, h)) for h in range(2)], rows, cols, s.pairs)
+
+
+def mix_chunk(c, s):
+    at = chunk_rows(c)
+    q, v = s.q[at], s.v[at]
+    first = s.first[at]
+    rows, cols = ([ref[i, at] for i in range(len(HALVES) + 1)] for ref in (s.rows, s.cols))
+    kv = s.enter[...]
+    low = kv.astype(BF)
+    s.kvs[c] = low
+    outer = jnp.concatenate([nt(head(q, h), state(low, h)[:, :DH]) for h in range(2)], 1)
+    logits = first * outer + s.logits[at]
+    s.logits[at] = logits
+    probs = softmax2(logits)
+    reading = back_through([probs], rows, cols, s.pairs)
+    spread = (probs * first).astype(BF)
+    s.enter[...] = s.fades[c, :, :1] * kv + s.adds[c]
+    code = s.code[at, :1]
+    for h in range(2):
+        mine = slice(h * DH, (h + 1) * DH)
+        mixed = dot(slots(spread, h), state(low, h)[:, DH:]) + dot(reading[h].astype(BF), head(v, h))
+        s.mixed[at, mine] = mixed
+        r = lax.rsqrt(jnp.mean(mixed * mixed, axis=-1, keepdims=True) + EPS)
+        s.normed[at, mine] = (mixed * jnp.where(code > 0.5, r, 0.0) * s.gain[:, mine]).astype(BF)
+
+
+def feed_rows(n, s):
+    at = pl.ds(n * WIDE, WIDE)
+    hn, cot = s.hidden[at], s.cot[at]
+    wide = s.wg.shape[1]
+    slot = n % 2
+    for c in range(0, wide, 512):
+        some = slice(c, min(c + 512, wide))
+        gate, up, dact = dot(hn, s.wg[:, some]), dot(hn, s.wu[:, some]), nt(cot, s.wd[some])
+        sig = 1.0 / (1.0 + jnp.exp(-gate))
+        soft = gate * sig
+        s.act[slot, :, some] = (soft * up).astype(BF)
+        s.dgate[slot, :, some] = (dact * up * sig * (1.0 + gate * (1.0 - sig))).astype(BF)
+        s.dup[slot, :, some] = (dact * soft).astype(BF)
+    s.dh[at] = (nt(s.dgate[slot], s.wg[...]) + nt(s.dup[slot], s.wu[...])).astype(BF)
+
+
+def front_kernel(sizes, *refs):
+    refs = list(refs)
+    take = lambda n: [refs.pop(0) for _ in range(n)]
+    lengths, tokens_own, cot_own = take(3)
+    sources, saves = take(len(FRONT_LOADED)), take(len(FRONT_SAVED))
+    hidden_out, cot_out, act_out, dgate_out, dup_out, dh_out, dh_got = take(7)
+    s = Bag()
+    for name in FRONT_LOADED + FRONT_SAVED:
+        setattr(s, name, refs.pop(0))
+    for name in ("tokens", "total", "fade", "enter", "reach", "sent", "got", "attn", "attn_got", "hidden", "cot", "act",
+                 "dgate", "dup", "first", "rows", "cols", "adds", "fades"):
+        setattr(s, name, refs.pop(0))
+    s.lengths = lengths
+    s.dh = s.xn
+    load_sem, save_sem, row_sem, part_sem = take(4)
+    scan_sems, swap_sems = take(2), take(2)
+    lines = Lines(sizes)
+    half, width = tokens_own.shape
+    count = 2 * half // CH
+    tp_peer = {"tp": 1 - lines.half}
+    own_rows = pl.ds(pl.multiple_of(lines.half * half, half), half)
+    loads = [pltpu.make_async_copy(x, getattr(s, n), load_sem.at[i]) for i, (n, x) in enumerate(zip(FRONT_LOADED, sources))]
+    late = loads[FRONT_LOADED.index("wo") :] + [pltpu.make_async_copy(cot_own, s.cot.at[pl.ds(0, half)], row_sem.at[1])]
+    loads = loads[: FRONT_LOADED.index("wo")] + [pltpu.make_async_copy(tokens_own, s.tokens.at[own_rows], row_sem.at[0])]
+    for copy in loads:
+        copy.start()
+    s.first_row = lines.index * (2 * half)
+    lines.greet()
+    tokens_swap = remote(tokens_own, s.tokens.at[own_rows], swap_sems, 0, tp_peer)
+    tokens_swap.start()
+    cot_swap = remote(cot_own, s.cot.at[pl.ds(half, half)], swap_sems, 1, tp_peer)
+    cot_swap.start()
+    for copy in late:
+        copy.start()
+    for copy in loads:
+        copy.wait()
+
+    def save(*names):
+        for n in names:
+            i = FRONT_SAVED.index(n)
+            pltpu.make_async_copy(getattr(s, n), saves[i], save_sem.at[i]).start()
+
+    for side in (lines.half, 1 - lines.half):
+        lax.fori_loop(0, half // WIDE, lambda i, carry: (project_rows(side * (half // WIDE) + i, s), carry)[1], 0)
+        if side is lines.half:
+            tokens_swap.wait()
+    total, fade = s.adds[0], s.fades[0]
+    for c in range(1, count):
+        total = s.fades[c, :, :1] * total + s.adds[c]
+        fade = fade * s.fades[c]
+    s.total[...], s.fade[...] = total, fade
+    early = ("code", "xn", "q", "k", "v", "dsq", "dsk", "gate", "weight", "dzf")
+    save(*early)
+
+    def between(n):
+        if n < 4:
+            for c in range(n * count // 4, (n + 1) * count // 4):
+                inner_chunk(c, s)
+
+    scans = scan_lines(lines, s.total, s.fade, s.enter, s.reach, s.sent, s.got, scan_sems, True, between)
+    lax.fori_loop(0, count, lambda c, carry: (mix_chunk(c, s), carry)[1], 0)
+    save("logits", "kvs", "mixed", "normed")
+
+    for copy in late:
+        copy.wait()
+    steps = half // WIDE
+    swaps = [
+        remote(s.attn.at[pl.ds(n * WIDE, WIDE)], s.attn_got.at[pl.ds(n * WIDE, WIDE)], swap_sems, 2 + n, tp_peer)
+        for n in range(steps)
+    ]
+    for n in range(2 * steps):
+        side = (1 - lines.half) if n < steps else lines.half
+        rows = pl.ds(pl.multiple_of(side * half + n % steps * WIDE, WIDE), WIDE)
+        s.attn[n * WIDE : (n + 1) * WIDE] = dot(s.normed[rows], s.wo[...]).astype(BF)
+        if n < steps:
+            swaps[n].start()
+    for n in range(steps):
+        at = pl.ds(n * WIDE, WIDE)
+        swaps[n].wait_recv()
+        attn = s.attn[half + n * WIDE : half + (n + 1) * WIDE].astype(F32) + s.attn_got[at].astype(F32)
+        x = s.tokens[pl.ds(pl.multiple_of(lines.half * half + n * WIDE, WIDE), WIDE)].astype(F32) + attn
+        s.resid[at] = x
+        r = lax.rsqrt(jnp.mean(x * x, axis=-1, keepdims=True) + EPS)
+        s.hidden[at] = (x * r * s.feed_gain[...]).astype(BF)
+        there = s.hidden.at[pl.ds(half + n * WIDE, WIDE)]
+        swaps.append(remote(s.hidden.at[at], there, swap_sems, 2 + steps + n, tp_peer))
+        swaps[-1].start()
+    save("resid")
+    cot_swap.wait()
+    cot_save = pltpu.make_async_copy(s.cot, cot_out, row_sem.at[2])
+    cot_save.start()
+
+    outs = ((s.act, act_out), (s.dgate, dgate_out), (s.dup, dup_out))
+    part = lambda n: [
+        pltpu.make_async_copy(src.at[n % 2], dst.at[pl.ds(n * WIDE, WIDE)], part_sem.at[n, i])
+        for i, (src, dst) in enumerate(outs)
+    ]
+    back = [
+        remote(s.dh.at[pl.ds(half + n * WIDE, WIDE)], dh_got.at[pl.ds(n * WIDE, WIDE)], swap_sems, 2 + 2 * steps + n, tp_peer)
+        for n in range(steps)
+    ]
+    busy = {}
+    at_xn = FRONT_SAVED.index("xn")
+    pltpu.make_async_copy(s.xn, saves[at_xn], save_sem.at[at_xn]).wait()
+    for n in [0] + list(range(steps, 2 * steps)) + list(range(1, steps)):
+        if n % 2 in busy:
+            for copy in busy[n % 2]:
+                copy.wait()
+        if n >= steps:
+            swaps[n].wait_recv()
+        feed_rows(n, s)
+        busy[n % 2] = part(n)
+        for copy in busy[n % 2]:
+            copy.start()
+        if n >= steps:
+            back[n - steps].start()
+    ends = [
+        pltpu.make_async_copy(s.hidden, hidden_out, row_sem.at[3]),
+        pltpu.make_async_copy(s.dh.at[pl.ds(0, half)], dh_out, row_sem.at[4]),
+    ]
+    for copy in ends:
+        copy.start()
+    for copy in ends + busy[0] + busy[1] + [cot_save]:
+        copy.wait()
+    for i, n in enumerate(FRONT_SAVED):
+        if i != at_xn:
+            pltpu.make_async_copy(getattr(s, n), saves[i], save_sem.at[i]).wait()
+    for copy in back:
+        copy.wait()
+    for copy in scans + swaps:
+        copy.wait_send()
+
+
+def front_call(lengths, tokens, cot, loaded):
+    sizes = line_sizes(lax.axis_size("seq"))
+    rounds = (sizes[0] * sizes[1] * sizes[2]).bit_length() - 1
+    half, width = tokens.shape
+    span = 2 * half
+    lanes, cols, hidden = (loaded[n].shape[1] for n in ("wf", "wq", "wg"))
+    levels = len(HALVES) + 1
+    shapes = dict(
+        code=((span, lanes), F32),
+        xn=((span, width), BF), q=((span, cols), BF), k=((span, cols), BF), v=((span, cols), BF), dsq=((span, cols), BF),
+        dsk=((span, cols), BF), gate=((span, lanes), F32), weight=((span, lanes), F32), dzf=((span, lanes), F32),
+        logits=((span, lanes), F32), kvs=((span // CH, lanes, 2 * DH), BF), mixed=((span, cols), F32),
+        normed=((span, cols), BF), resid=((half, width), F32),
+    )
+    others = [
+        ((span, width), BF), ((lanes, 2 * DH), F32), ((lanes, CH), F32), ((lanes, 2 * DH), F32), ((lanes, CH), F32),
+        ((rounds, lanes + TAIL, 2 * DH), BF), ((rounds, lanes + TAIL, 2 * DH), BF), ((span, width), BF), ((half, width), BF),
+        ((span, width), BF), ((span, width), BF), ((2, WIDE, hidden), BF), ((2, WIDE, hidden), BF), ((2, WIDE, hidden), BF),
+        ((span, lanes), F32), ((levels, span, lanes), F32), ((levels, span, lanes), BF),
+        ((span // CH, lanes, 2 * DH), F32), ((span // CH, lanes, CH), F32),
+    ]
+    more = [((span, width), BF)] * 2 + [((span, hidden), BF)] * 3 + [((half, width), BF)] * 2
+    dma = pltpu.SemaphoreType.DMA
+    scratch = [pltpu.VMEM(loaded[n].shape, loaded[n].dtype) for n in FRONT_LOADED]
+    scratch += [pltpu.VMEM(*shapes[n]) for n in FRONT_SAVED] + [pltpu.VMEM(*x) for x in others]
+    scratch += [dma((len(FRONT_LOADED),)), dma((len(FRONT_SAVED),)), dma((5,)), dma((span // WIDE, 3))]
+    scratch += [dma((rounds,))] * 2 + [dma((2 + 3 * (half // WIDE),))] * 2
+    anywhere = pl.BlockSpec(memory_space=pl.ANY)
+    outs = pl.pallas_call(
+        functools.partial(front_kernel, sizes),
+        out_shape=[jax.ShapeDtypeStruct(*x) for x in [shapes[n] for n in FRONT_SAVED] + more],
+        in_specs=[pl.BlockSpec(memory_space=pltpu.SMEM)] + [anywhere] * (2 + len(FRONT_LOADED)),
+        out_specs=[anywhere] * (len(FRONT_SAVED) + len(more)),
+        scratch_shapes=scratch,
+        compiler_params=pltpu.CompilerParams(collective_id=1, has_side_effects=True, vmem_limit_bytes=63 * 1024 * 1024),
+        name="front",
+    )(lengths, tokens, cot, *[loaded[n] for n in FRONT_LOADED])
     return dict(zip(FRONT_SAVED, outs)), outs[len(FRONT_SAVED) :]
 
 
@@ -1083,18 +1432,6 @@
 )
 
 
-def token_code(lengths, positions):
-    buckets = (lengths + BUCKET - 1) // BUCKET
-    spans = buckets * BUCKET
-    starts = jnp.cumsum(spans) - spans
-    segment = jnp.sum((positions[:, None] >= starts[None, :]).astype(jnp.int32), axis=1) - 1
-    picked = segment[:, None] == jnp.arange(lengths.shape[0], dtype=jnp.int32)[None, :]
-    begin = jnp.sum(jnp.where(picked, starts[None, :], 0), axis=1)
-    length = jnp.sum(jnp.where(picked, lengths[None, :], 0), axis=1)
-    offset = positions - begin
-    return jnp.where(offset == 0, 2.0, jnp.where(offset < length, 1.0, 0.0)).astype(F32)
-
-
 def per_device(
     tokens, norm_gain, query_weight, key_weight, value_weight, forget_weight, forget_bias, head_gain,
     out_weight, feed_gain, gate_weight, up_weight, down_weight, lengths, cotangent,
@@ -1107,18 +1444,16 @@
     sums, back = jnp.asarray(sums, BF), jnp.asarray(back, BF)
     pairs, flipped = jnp.asarray(pairs, BF), jnp.asarray(flipped, BF)
 
-    positions = lax.axis_index("seq") * span + jnp.arange(span, dtype=jnp.int32)
-    code = jnp.broadcast_to(token_code(lengths, positions)[:, None], (span, lanes))
     weights = dict(wq=query_weight, wk=key_weight, wv=value_weight, wf=forget_weight, wo=out_weight)
-    shared = dict(code=code, sums=sums, pairs=pairs, gain=head_gain[None], norm_gain=norm_gain[None])
+    shared = dict(sums=sums, pairs=pairs, gain=head_gain[None], norm_gain=norm_gain[None])
     wide = dict(wg=gate_weight, wu=up_weight, wd=down_weight, bias=forget_bias[None], feed_gain=feed_gain[None])
-    saved, (hidden, cot, act, dgate, dup, dh_own, dh_got) = front_call(tokens, cotangent, dict(weights, **shared, **wide))
+    saved, (hidden, cot, act, dgate, dup, dh_own, dh_got) = front_call(lengths, tokens, cotangent, dict(weights, **shared, **wide))
     resid = saved["resid"]
     loaded = dict(weights, **shared, flipped=flipped, back=back, feed_gain=feed_gain[None])
-    for name in ("q", "k", "v", "dsq", "dsk", "gate", "weight", "dzf", "logits", "kvs", "mixed", "normed"):
+    for name in ("code", "q", "k", "v", "dsq", "dsk", "gate", "weight", "dzf", "logits", "kvs", "mixed", "normed"):
         loaded[name] = saved[name]
     rows = (dh_own, dh_got, act, cot, hidden, dgate, dup, down_weight, resid, tokens, saved["xn"])
-    gains, bias_sum, head_sum, block_out, tokens_grad, _, _, _, *sums = back_call(rows, loaded, JOBS, TICKS, PIECES)
+    norm_sum, feed_sum, bias_sum, head_sum, block_out, tokens_grad, _, _, _, *sums = back_call(rows, loaded, JOBS, TICKS, PIECES)
     ff_sum, down_sum, mixer_sum, out_sum = sums
     blocks, ff_blocks, wide = cols // 128, gate_weight.shape[1] // 128, tuple(range(width // 128))
     which = lambda up: tuple(4 * (c // 2) + 2 * up + c % 2 - (up if c == ff_blocks - 1 else 0) for c in range(ff_blocks))
@@ -1127,8 +1462,8 @@
     arrays = [mixer_sum, out_sum.reshape(-1, cols, 128), ff_sum, down_sum.reshape(-1, down_weight.shape[0], 128)]
     query_sum, key_sum, value_sum, forget_sum, out_grad, gate_grad, up_grad, down_grad = widen(arrays, parts, 8)
     return (
-        block_out, tokens_grad, gains[0], query_sum, key_sum, value_sum, forget_sum, bias_sum[0], head_sum[0], out_grad,
-        gains[1], gate_grad, up_grad, down_grad,
+        block_out, tokens_grad, norm_sum[0], query_sum, key_sum, value_sum, forget_sum, bias_sum[0], head_sum[0], out_grad,
+        feed_sum[0], gate_grad, up_grad, down_grad,
     )
 
 

time: 346 us -> 332 us (0.960)
  Pallas kernels: 332 us -> 320 us
    pallas_call x1, Pallas kernels: 76.6 us -> 68.9 us  [front_call(): pl.pallas_call(functools.partial(front_kernel, sizes), out_shape=[jax.Sha...]
    pallas_call x1, Pallas kernels: 241 us -> 237 us  [back_call(): pl.pallas_call(functools.partial(back_kernel, sizes, jobs, ticks, pieces)...]
where the time goes in v1:
time: 332 us; the launch traced here: 325 us
  Pallas kernels  320 us (96%)
  local copies, waits for them, and re-layouts  4.25 us (1%)
    pallas_call x1, Pallas kernels, back_call(): pl.pallas_call(functools.partial(back_kernel, sizes, jobs, ticks, pieces)...  237 us
    pallas_call x1, Pallas kernels, front_call(): pl.pallas_call(functools.partial(front_kernel, sizes), out_shape=[jax.Sha...  68.9 us
    pallas_call x1, Pallas kernels, widen(): pl.pallas_call(functools.partial(widen_kernel, parts), grid=(steps,), in_...  14.5 us

profile of v1, /device:TPU:0, one launch (start us, length us, event | category | flops | bytes accessed | tf_op | source)
XLA Modules:
  0.0 325.1 jit_solution(6742516065154117272)
XLA Ops:
  0.6 68.9 %front.1 = (f32[1024,128]{1,0:T(8,128)}, bf16[1024,1024]{1,0:T(8,128)(2,1)}, bf16[1024,512]{1,0:T(8,128)(2,1)}, bf16[1024,512]{1,0:T(8,128)(2,1)}, bf16[1024,512...) custom-call(s32[4]{0:T(128)} %refs_0_.1, ...), custom_call_target="tpu_custom_call" | custom-call | tf_op jit(solution)/shard_map/front/pallas_call | solution.py:1373
  69.5 236.7 %back.1 = (f32[1,1024]{1,0:T(1,128)}, f32[1,1024]{1,0:T(1,128)}, f32[1,128]{1,0:T(1,128)}, f32[1,512]{1,0:T(1,128)}, bf16[512,1024]{1,0:T(8,128)(2,1)}, /*index=...) custom-call(bf16[512,1024]{1,0:T(8,128)(2,1)} %get-tuple-element.54., ...), custom_call_target="tpu_custom_call" | custom-call | tf_op jit(solution)/shard_map/back/pallas_call | solution.py:787
  306.2 0.0 copy-start.1
  306.2 0.0 copy-start
  306.2 14.5 %widen.1 = (f32[1024,512]{1,0:T(8,128)}, f32[1024,512]{1,0:T(8,128)}, f32[1024,512]{1,0:T(8,128)}, f32[1024,128]{1,0:T(8,128)}, f32[512,1024]{1,0:T(8,128)}, /*i...) custom-call(bf16[13,1024,128]{2,1,0:T(8,128)(2,1)} %get-tuple-element.79.refs_0_, ...), custom_call_target="tpu_custom_call" | custom-call | tf_op jit(solution)/shard_map/widen/pallas_call | solution.py:1392
  320.7 0.0 copy-start.3
  320.7 0.0 copy-start.5
  320.7 0.0 copy-start.4
  320.7 0.0 copy-start.2
  320.7 0.0 copy-done.1
  320.7 1.0 copy.39
  321.7 0.0 copy-done
  321.7 1.0 copy.40
  322.7 0.0 copy-done.3
  322.7 0.6 copy.41
  323.3 0.0 copy-done.5
  323.3 0.5 copy.42
  323.8 0.0 copy-done.4
  323.8 0.6 copy.43
  324.4 0.0 copy-done.2
  324.4 0.6 copy.44
Async XLA Ops:
  306.2 14.5 %copy-start.1 = (bf16[512,1024]{1,0:T(8,128)(2,1)S(1)}, bf16[512,1024]{1,0:T(8,128)(2,1)}, u32[]{:S(2)}) copy-start(bf16[512,1024]{1,0:T(8,128)(2,1)} %get-tuple-element.108) | copy-start | bytes 3145732
  306.2 15.5 %copy-start = (bf16[512,1024]{1,0:T(8,128)(2,1)S(1)}, bf16[512,1024]{1,0:T(8,128)(2,1)}, u32[]{:S(2)}) copy-start(bf16[512,1024]{1,0:T(8,128)(2,1)} %get-tuple-element.109) | copy-start | bytes 3145732
  320.7 2.0 copy-start.3
  320.7 2.6 copy-start.5
  320.7 3.1 copy-start.4
  320.7 3.7 %copy-start.2 = (f32[1,1024]{1,0:T(1,128)S(1)}, f32[1,1024]{1,0:T(1,128)}, u32[]{:S(2)}) copy-start(f32[1,1024]{1,0:T(1,128)} %get-tuple-element.90) | copy-start | bytes 12292
